TPU v7x, 512 devices: a whole 4x8x8 slice. The times are simulated.
512 devices in a mesh: source: 8 (over y_hi, core), cand: 8 (over x, y_lo), tensor: 8 (over z).
Axes of the slice: x: 4, y: 8 (y_hi: 4, y_lo: 2; y = y_hi * 2 + y_lo), z: 8, core: 2. Of those that a mesh axis runs over, the one named last changes fastest.
Arguments:
- dec_states: bfloat16 [8, 8, 128, 4096], P('source', 'cand', None, 'tensor'), may hold values from -6 to 6
- enc_states: bfloat16 [8, 96, 4096], P('source', None, 'cand'), may hold values from -6 to 6
- norm_gain: float32 [4096], replicated, may hold values from 0.5 to 1.5
- w_query: bfloat16 [4096, 2048], P('cand', 'tensor'), may hold values from -0.09375 to 0.09375
- w_key: bfloat16 [4096, 2048], P('cand', 'tensor'), may hold values from -0.09375 to 0.09375
- w_value: bfloat16 [4096, 2048], P('cand', 'tensor'), may hold values from -0.09375 to 0.09375
- w_out: bfloat16 [2048, 4096], P('tensor', 'cand'), may hold values from -0.125 to 0.125
- target_rows: bfloat16 [8, 8, 128, 4096], P('source', 'cand'), may hold values from -6 to 6
- cand_lengths: int32 [8, 8], P('source', 'cand'), may hold values from 1 to 128, 640 in all within a row
- src_lengths: int32 [8], P('source'), may hold values from 1 to 96, 576 in all
- costs: int32 [8, 8], P('source', 'cand'), may hold values from 0 to 100
Outputs:
- loss: float32 [], replicated
- grad_dec: float32 [8, 8, 128, 4096], P('source', 'cand', None, 'tensor')
- grad_enc: float32 [8, 96, 4096], P('source', 'tensor', 'cand')
- radial_grad: float32 [8, 8, 128], P('source', 'cand')
Inputs may be any that keep to these rules, and one draw needn't show every extreme that they name: `cand_lengths`: for each source the 8 lengths sum to 640 and the longest is exactly 128. `src_lengths`: the 8 lengths sum to 576 and the longest is exactly 96.
All inputs are finite; a program needn't handle non-finite values. No bound on the sum of `cand_lengths` or of `src_lengths` on one device may be relied on, other than what follows from the above.
Results may differ from a plain program's by a relative error of at most 0.033.
Values may be sent and summed in bfloat16 or wider, within the bound.
A program may use at most 64 MiB of HBM per device.

v0:
```python
import jax
import jax.numpy as jnp
from jax import lax
from jax.sharding import PartitionSpec as P

HEAD_DIM = 64


def contract_last(left, right):
    return lax.dot_general(
        left, right, (((1,), (1,)), ((), ())), preferred_element_type=jnp.float32
    )


def local(
    dec_states,
    enc_states,
    norm_gain,
    w_query,
    w_key,
    w_value,
    w_out,
    target_rows,
    cand_lengths,
    src_lengths,
    costs,
):
    scale = HEAD_DIM ** (-0.5)
    local_x = dec_states[0, 0]
    slice_w = local_x.shape[1]
    tindex = lax.axis_index("tensor")
    full_x = lax.all_gather(local_x, "tensor", axis=1, tiled=True).astype(jnp.float32)
    width = full_x.shape[1]
    inv_rms = lax.rsqrt(jnp.mean(full_x * full_x, axis=1, keepdims=True) + 1e-06)
    normed = (full_x * inv_rms * norm_gain).astype(jnp.bfloat16)
    enc_local = enc_states[0]
    query_w, key_w, value_w = (
        lax.all_gather(w_query, "cand", axis=0, tiled=True),
        lax.all_gather(w_key, "cand", axis=0, tiled=True),
        lax.all_gather(w_value, "cand", axis=0, tiled=True),
    )
    enc_full = lax.all_gather(enc_local, "cand", axis=1, tiled=True)
    key_f = jnp.dot(enc_full, key_w, preferred_element_type=jnp.float32)
    value_f = jnp.dot(enc_full, value_w, preferred_element_type=jnp.float32)
    keys = key_f.astype(jnp.bfloat16)
    values = value_f.astype(jnp.bfloat16)
    query = jnp.dot(normed, query_w, preferred_element_type=jnp.float32).astype(jnp.bfloat16)
    tgt = query.shape[0]
    src = keys.shape[0]
    heads = query.shape[1] // HEAD_DIM
    q_three = query.reshape(tgt, heads, HEAD_DIM)
    k_three = keys.reshape(src, heads, HEAD_DIM)
    v_three = values.reshape(src, heads, HEAD_DIM)
    key_mask = (jnp.arange(src) < src_lengths[0]).astype(jnp.float32)
    logits = (
        jnp.einsum("thd,shd->hts", q_three, k_three, preferred_element_type=jnp.float32) * scale
    )
    expo = jnp.exp(logits) * key_mask
    probs_f = expo / jnp.sum(expo, axis=2, keepdims=True)
    probs = probs_f.astype(jnp.bfloat16)
    context = (
        jnp.einsum("hts,shd->thd", probs, v_three, preferred_element_type=jnp.float32)
        .astype(jnp.bfloat16)
        .reshape(tgt, heads * HEAD_DIM)
    )
    out_w = lax.all_gather(w_out, "cand", axis=1, tiled=True)
    term = jnp.dot(context, out_w, preferred_element_type=jnp.float32)
    length_f = cand_lengths[0, 0].astype(jnp.float32)
    tok_mask = (jnp.arange(tgt) < cand_lengths[0, 0]).astype(jnp.float32)
    factor = tok_mask / jnp.sqrt(width * length_f)
    rows = target_rows[0, 0]
    x_part = local_x.astype(jnp.float32)
    attn = lax.psum(term.astype(jnp.bfloat16), "tensor").astype(jnp.float32)
    out_full = full_x + attn
    score = jnp.sum(jnp.sum(out_full * rows.astype(jnp.float32), axis=1) * factor)
    risk = costs[0, 0].astype(jnp.float32) / 100.0
    weight = jnp.exp(score)
    total_w, total_wr = lax.psum((weight, weight * risk), "cand")
    expected = total_wr / total_w
    sources = lax.axis_size("source")
    loss = lax.psum(expected, "source") / sources
    grad_score = weight / total_w * (risk - expected) / sources
    coef = (grad_score * factor)[:, None]
    grad_out = (coef * rows.astype(jnp.float32)).astype(jnp.bfloat16)
    grad_out_part = lax.dynamic_slice_in_dim(grad_out, tindex * slice_w, slice_w, 1)
    grad_ctx = contract_last(grad_out, out_w).astype(jnp.bfloat16)
    gc_three = grad_ctx.reshape(tgt, heads, HEAD_DIM)
    grad_probs = jnp.einsum("thd,shd->hts", gc_three, v_three, preferred_element_type=jnp.float32)
    grad_logits = (
        probs_f * (grad_probs - jnp.sum(probs_f * grad_probs, axis=2, keepdims=True)) * scale
    ).astype(jnp.bfloat16)
    grad_query = (
        jnp.einsum("hts,shd->thd", grad_logits, k_three, preferred_element_type=jnp.float32)
        .astype(jnp.bfloat16)
        .reshape(tgt, heads * HEAD_DIM)
    )
    grad_key = (
        jnp.einsum("hts,thd->shd", grad_logits, q_three, preferred_element_type=jnp.float32)
        .astype(jnp.bfloat16)
        .reshape(src, heads * HEAD_DIM)
    )
    grad_value = (
        jnp.einsum("hts,thd->shd", probs, gc_three, preferred_element_type=jnp.float32)
        .astype(jnp.bfloat16)
        .reshape(src, heads * HEAD_DIM)
    )
    grad_normed = contract_last(grad_query, query_w)
    normed_part = lax.psum_scatter(
        grad_normed.astype(jnp.bfloat16), "tensor", scatter_dimension=1, tiled=True
    ).astype(jnp.float32)
    gain_part = lax.dynamic_slice_in_dim(norm_gain, tindex * slice_w, slice_w)
    inner = lax.psum(jnp.sum(gain_part * normed_part * x_part, axis=1), "tensor")
    grad_dec = (
        grad_out_part.astype(jnp.float32)
        + inv_rms * gain_part * normed_part
        - x_part * inv_rms**3 * inner[:, None] / width
    )
    radial_grad = inner / jnp.sqrt(jnp.float32(width))
    enc_term = contract_last(grad_key, key_w) + contract_last(grad_value, value_w)
    enc_rows = lax.psum_scatter(
        enc_term.astype(jnp.bfloat16), "tensor", scatter_dimension=0, tiled=True
    )
    grad_enc = lax.psum_scatter(enc_rows, "cand", scatter_dimension=1, tiled=True).astype(
        jnp.float32
    )
    return (loss, grad_dec[None, None], grad_enc[None], radial_grad[None, None])


def solution(mesh):
    placed = (
        P("source", "cand", None, "tensor"),
        P("source", None, "cand"),
        P(),
        P("cand", "tensor"),
        P("cand", "tensor"),
        P("cand", "tensor"),
        P("tensor", "cand"),
        P("source", "cand", None, None),
        P("source", "cand"),
        P("source"),
        P("source", "cand"),
    )
    return jax.shard_map(
        local,
        mesh=mesh,
        in_specs=placed,
        out_specs=(
            P(),
            P("source", "cand", None, "tensor"),
            P("source", "tensor", "cand"),
            P("source", "cand", None),
        ),
        check_vma=False,
    )
```

profile of v0, /device:TPU:6, one launch (start us, length us, event | category | flops | bytes accessed | tf_op | source)
XLA Modules:
  0.0 555.5 jit_solution(5566927231332925084)
XLA Ops:
  7.2 0.0 all-gather.16.cloned.1.call-start
  7.2 0.7 all-gather.16.cloned.1.call-update
  7.9 0.0 all-gather.10.cloned.1.call-start
  8.0 0.7 all-gather.10.cloned.1.call-update
  8.7 0.0 all-gather.12.cloned.1.call-start
  8.7 0.7 all-gather.12.cloned.1.call-update
  9.4 0.0 all-gather.8.cloned.1.call-start
  9.4 0.5 all-gather.8.cloned.1.call-update
  10.0 0.0 all-gather.14.cloned.1.call-start
  10.0 0.5 all-gather.14.cloned.1.call-update
  10.6 0.0 all-reduce.5.cloned.1.call-start
  11.3 34.1 %all-gather.1 = bf16[1,96,4096]{2,1,0:T(8,128)(2,1)S(1)} all-gather(bf16[1,96,512]{2,1,0:T(8,128)(2,1)} %param.12), channel_id=3, replica_groups=mesh['source'=8,'cand'=8,'tensor'=8] {'cand'}, dimensions={2}, use_global_device_ids=true | all-gather | bytes 884736 | tf_op jit(solution)/shard_map/all_gather | solution.py:42
  45.3 11.6 %all-gather.16.cloned.1.call-done = bf16[1,1,128,4096]{3,2,1,0:T(8,128)(2,1)} async-done(((bf16[1,1,128,512]{3,2,1,0:T(8,128)(2,1)}), bf16[1,1,128,4096]{3,2,1,0:T(8,128)(2,1)}) %all-gather.16.cloned.1.call-update) | async-done | bytes 1048592 | tf_op jit(solution)/shard_map/all_gather | solution.py:32
  56.9 1.5 fusion.5
  58.4 54.4 %all-gather.10.cloned.1.call-done = bf16[4096,256]{1,0:T(8,128)(2,1)} async-done(((bf16[512,256]{1,0:T(8,128)(2,1)}), bf16[4096,256]{1,0:T(8,128)(2,1)}) %all-gather.10.cloned.1.call-update) | async-done | bytes 2097168 | tf_op jit(solution)/shard_map/all_gather | solution.py:38
  112.9 2.4 convolution_convert_fusion.3
  115.3 0.1 copy.30
  115.4 56.3 %all-gather.12.cloned.1.call-done = bf16[4096,256]{1,0:T(8,128)(2,1)} async-done(((bf16[512,256]{1,0:T(8,128)(2,1)}), bf16[4096,256]{1,0:T(8,128)(2,1)}) %all-gather.12.cloned.1.call-update) | async-done | bytes 2097168 | tf_op jit(solution)/shard_map/all_gather | solution.py:39
  171.7 2.1 convolution_convert_fusion.8
  173.8 0.1 copy.31
  173.9 56.5 %all-gather.8.cloned.1.call-done = bf16[4096,256]{1,0:T(8,128)(2,1)} async-done(((bf16[512,256]{1,0:T(8,128)(2,1)}), bf16[4096,256]{1,0:T(8,128)(2,1)}) %all-gather.8.cloned.1.call-update) | async-done | bytes 2097168 | tf_op jit(solution)/shard_map/all_gather | solution.py:40
  230.4 2.1 convolution_convert_fusion.9
  232.5 0.1 copy.29
  232.6 0.2 fusion.12
  232.9 0.2 convolution_convert_fusion.7
  233.1 56.1 %all-gather.14.cloned.1.call-done = bf16[256,4096]{1,0:T(8,128)(2,1)} async-done(((bf16[256,512]{1,0:T(8,128)(2,1)}), bf16[256,4096]{1,0:T(8,128)(2,1)}) %all-gather.14.cloned.1.call-update) | async-done | bytes 2097168 | tf_op jit(solution)/shard_map/all_gather | solution.py:66
  289.2 3.2 convolution_convert_fusion.1
  292.4 0.0 all-reduce.5.cloned.1.call-update
  292.4 0.0 reduce-scatter.7.cloned.1.call-start
  293.8 1.3 dynamic-slice.4
  295.7 80.0 %all-reduce.5.cloned.1.call-done = bf16[128,4096]{1,0:T(8,128)(2,1)} async-done(((bf16[128,4096]{1,0:T(8,128)(2,1)}), bf16[128,4096]{1,0:T(8,128)(2,1)}) %all-reduce.5.cloned.1.call-update) | async-done | bytes 1048592 | tf_op jit(solution)/shard_map/psum | solution.py:73
  375.7 1.7 fusion.3
  377.4 0.6 multiply_reduce_fusion.1
  378.7 0.9 fusion.31
  379.7 16.8 %all-reduce.2 = (f32[]{:T(128)}, f32[]{:T(128)}) all-reduce(f32[]{:T(128)S(6)} %mul.128, f32[]{:T(128)S(6)} %exp.7), channel_id=1, replica_groups=mesh['source'=8,'cand'=8,'tensor'=8] {'cand'}, use_global_device_ids=true, to_apply=%region_5.0 | all-reduce | flops 2 | bytes 16 | tf_op jit(solution)/shard_map/psum | solution.py:78
  398.4 0.3 fusion.4
  398.7 2.6 convolution_convert_fusion.2
  401.3 0.1 copy.32
  401.4 0.9 fusion.44
  402.3 1.2 convolution_convert_fusion.4
  403.5 1.4 convolution_convert_fusion.5
  405.0 0.8 fusion.45
  405.7 0.8 copy-done.1
  406.5 0.8 fusion.2
  407.3 21.7 %fusion = bf16[16,4096]{1,0:T(8,128)(2,1)S(1)} fusion(bf16[96,4096]{1,0:T(8,128)(2,1)S(1)} %fusion.2), kind=kCustom, calls=%all-reduce-scatter | all-reduce-scatter fusion | flops 524289 | bytes 919552
  429.1 3.3 collective-permute-start
  432.4 3.8 collective-permute-start.1
  436.2 1.4 convolution_convert_fusion.6
  437.6 1.1 collective-permute-done.1
  438.7 0.6 concatenate
  439.3 0.7 constant_dynamic-slice_fusion
  440.0 0.0 reduce-scatter.7.cloned.1.call-update
  440.0 0.0 reduce-scatter.5.cloned.1.call-start
  440.1 3.4 convolution_convert_fusion
  443.6 0.1 dynamic_slice.7
  443.6 14.7 %psum.38 = f32[]{:T(128)} all-reduce(f32[]{:T(128)S(6)} %div.57), channel_id=1, replica_groups=mesh['source'=8,'cand'=8,'tensor'=8] {'source'}, use_global_device_ids=true, to_apply=%region_7.0 | all-reduce | flops 1 | bytes 8 | tf_op jit(solution)/shard_map/psum | solution.py:81
  459.0 24.6 %reduce-scatter.7.cloned.1.call-done = bf16[12,512]{1,0:T(8,128)(2,1)} async-done(((bf16[12,4096]{1,0:T(8,128)(2,1)}), bf16[12,512]{1,0:T(8,128)(2,1)}) %reduce-scatter.7.cloned.1.call-update) | async-done | bytes 12304 | tf_op jit(solution)/shard_map/reduce_scatter | solution.py:123
  483.6 0.7 bitcast_convert_fusion
  484.3 0.6 copy.33
  485.0 43.9 %reduce-scatter.5.cloned.1.call-done = bf16[128,512]{1,0:T(8,128)(2,1)} async-done(((bf16[128,4096]{1,0:T(8,128)(2,1)}), bf16[128,512]{1,0:T(8,128)(2,1)}) %reduce-scatter.5.cloned.1.call-update) | async-done | bytes 131088 | tf_op jit(solution)/shard_map/reduce_scatter | solution.py:108
  528.8 1.0 fusion.29
  529.8 15.3 %psum.39 = f32[128]{0:T(128)S(1)} all-reduce(f32[128]{0:T(128)S(1)} %fusion.29), channel_id=1, replica_groups=mesh['source'=8,'cand'=8,'tensor'=8] {'tensor'}, use_global_device_ids=true, to_apply=%region_11.0 | all-reduce | flops 128 | bytes 1024 | tf_op jit(solution)/shard_map/psum | solution.py:112
  545.2 0.5 multiply_bitcast_fusion
  545.7 1.8 fusion.26
  (19 shorter events, 0.1 us)
Async XLA Ops:
  7.2 105.7 %copy-start.6 = (f32[4096]{0:T(1024)S(1)}, f32[4096]{0:T(1024)}, u32[]{:S(2)}) copy-start(f32[4096]{0:T(1024)} %param.13) | copy-start | bytes 49156
  7.2 49.7 %all-gather.16.cloned.1.call-start = ((), (), s32[]{:S(2)}) async-start(), calls=%async_computation.9 | async-start | bytes 1179648 | tf_op jit(solution)/shard_map/all_gather | solution.py:32
  7.9 105.0 %all-gather.10.cloned.1.call-start = ((), (), s32[]{:S(2)}) async-start(), calls=%async_computation.3 | async-start | bytes 2359296 | tf_op jit(solution)/shard_map/all_gather | solution.py:38
  8.7 163.1 %all-gather.12.cloned.1.call-start = ((), (), s32[]{:S(2)}) async-start(), calls=%async_computation.4 | async-start | bytes 2359296 | tf_op jit(solution)/shard_map/all_gather | solution.py:39
  9.4 221.1 %all-gather.8.cloned.1.call-start = ((), (), s32[]{:S(2)}) async-start(), calls=%async_computation.2 | async-start | bytes 2359296 | tf_op jit(solution)/shard_map/all_gather | solution.py:40
  10.0 279.2 %all-gather.14.cloned.1.call-start = ((), (), s32[]{:S(2)}) async-start(), calls=%async_computation.5 | async-start | bytes 2359296 | tf_op jit(solution)/shard_map/all_gather | solution.py:66
  10.6 365.2 %all-reduce.5.cloned.1.call-start = ((), (), s32[]{:S(2)}) async-start(), calls=%async_computation.6 | async-start | bytes 2097152 | tf_op jit(solution)/shard_map/psum | solution.py:73
  232.9 56.3 %copy-start.5 = (f32[4,128,96]{1,2,0:T(8,128)}, f32[4,128,96]{1,2,0:T(8,128)S(1)}, u32[]{:S(2)}) copy-start(f32[4,128,96]{1,2,0:T(8,128)S(1)} %fusion.12) | copy-start | bytes 589828
  289.2 86.6 %copy-start.2 = (bf16[1,1,128,4096]{3,2,1,0:T(8,128)(2,1)S(1)}, bf16[1,1,128,4096]{3,2,1,0:T(8,128)(2,1)}, u32[]{:S(2)}) copy-start(bf16[1,1,128,4096]{3,2,1,0:T(8,128)(2,1)} %param.18) | copy-start | bytes 3145732
  289.2 86.6 %copy-start.3 = (bf16[1,1,128,4096]{3,2,1,0:T(8,128)(2,1)S(1)}, bf16[1,1,128,4096]{3,2,1,0:T(8,128)(2,1)}, u32[]{:S(2)}) copy-start(bf16[1,1,128,4096]{3,2,1,0:T(8,128)(2,1)} %all-gather.16.cloned.1.call-done) | copy-start | bytes 3145732
  292.4 191.2 %reduce-scatter.7.cloned.1.call-start = ((), (), s32[]{:S(2)}) async-start(), calls=%async_computation.8 | async-start | bytes 147456 | tf_op jit(solution)/shard_map/reduce_scatter | solution.py:123
  398.7 6.3 %copy-start = (bf16[4096,256]{1,0:T(8,128)(2,1)S(1)}, bf16[4096,256]{1,0:T(8,128)(2,1)}, u32[]{:S(2)}) copy-start(bf16[4096,256]{1,0:T(8,128)(2,1)} %all-gather.12.cloned.1.call-done) | copy-start | bytes 6291460
  404.9 1.6 copy-start.1
  429.1 9.6 %collective-permute-start = (bf16[16,4096]{1,0:T(8,128)(2,1)S(1)}, bf16[16,4096]{1,0:T(8,128)(2,1)S(1)}, u32[]{:S(2)}, u32[]{:S(2)}) collective-permute-start(bf16[16,4096]{1,0:T(8,128)(2,1)S(1)} %fusion), channel_id=1, source_target_pairs={{0,1},{1,2},{2,3},{3,4},{4,5},{5,6},{6,7},{8,9},{9,10},{10,11},{11... | collective-permute-start | bytes 393224
  432.4 6.3 %collective-permute-start.1 = (bf16[12,4096]{1,0:T(8,128)(2,1)S(1)}, bf16[12,4096]{1,0:T(8,128)(2,1)S(1)}, u32[]{:S(2)}, u32[]{:S(2)}) collective-permute-start(bf16[12,4096]{1,0:T(8,128)(2,1)S(1)} %slice), channel_id=1, source_target_pairs={{0,2},{1,3},{2,4},{3,5},{4,6},{5,7},{8,10},{9,11},{10,12},{11,13},... | collective-permute-start | bytes 294920
  440.0 88.8 %reduce-scatter.5.cloned.1.call-start = ((), (), s32[]{:S(2)}) async-start(), calls=%async_computation.7 | async-start | bytes 1179648 | tf_op jit(solution)/shard_map/reduce_scatter | solution.py:108
  440.1 88.7 %copy-start.4 = (bf16[1,1,128,512]{3,2,1,0:T(8,128)(2,1)S(1)}, bf16[1,1,128,512]{3,2,1,0:T(8,128)(2,1)}, u32[]{:S(2)}) copy-start(bf16[1,1,128,512]{3,2,1,0:T(8,128)(2,1)} %param.11) | copy-start | bytes 393220
Sparse Core Ops, SparseCore 0:
  10.1 46.7 all-gather.15
  59.0 53.8 all-gather.9
  115.0 56.7 all-gather.11
  173.7 56.7 all-gather.7
  232.4 56.7 all-gather.13
  292.5 83.1 all-reduce.4
  440.2 43.4 reduce-scatter.6
  486.7 42.1 reduce-scatter.4
where the time goes:
time: 556 us; the launch traced here: 555 us
  waiting for transfers between devices  388 us (70%)
  blocking collectives  103 us (19%)
  matrix products  23.6 us (4%)
  between operations  21.3 us (4%)
  other arithmetic  8.18 us (1%)
  starting transfers between devices  7.4 us (1%)
    psum x1, waiting for transfers between devices, local(): attn = lax.psum(term.astype(jnp.bfloat16), 'tensor').astype(jnp.float32)  80 us
    all_gather x1, waiting for transfers between devices, local(): lax.all_gather(w_value, 'cand', axis=0, tiled=True)  56.5 us
    all_gather x1, waiting for transfers between devices, local(): lax.all_gather(w_key, 'cand', axis=0, tiled=True)  56.3 us
    all_gather x1, waiting for transfers between devices, local(): out_w = lax.all_gather(w_out, 'cand', axis=1, tiled=True)  56.1 us
    all_gather x1, waiting for transfers between devices, local(): lax.all_gather(w_query, 'cand', axis=0, tiled=True)  54.4 us
    reduce_scatter x1, waiting for transfers between devices, local(): lax.psum_scatter(grad_normed.astype(jnp.bfloat16), 'tensor', scatter_dime...  43.9 us
    all_gather x1, blocking collectives, local(): enc_full = lax.all_gather(enc_local, 'cand', axis=1, tiled=True)  34.1 us
    reduce_scatter x1, waiting for transfers between devices, local(): lax.psum_scatter(enc_rows, 'cand', scatter_dimension=1, tiled=True)  24.6 us
  transfers between devices with their start and end apart: 10, of which 9 were waited for; matrix products, arithmetic and copies ran while one was open for 3% of the time, Pallas kernels for 0%

commit v1 on v0

v1 whole, which is shorter than its diff:
```python
import jax
import jax.numpy as jnp
from jax import lax
from jax.experimental import pallas as pl
from jax.experimental.pallas import tpu as pltpu
from jax.sharding import PartitionSpec as P

HEAD_DIM = 64
N = 8
XS = 4
CH = 4
MESH = pl.DeviceIdType.MESH
BF = jnp.bfloat16
F32 = jnp.float32


def dot(left, right):
    return jnp.dot(left, right, preferred_element_type=F32)


def dot_tt(left, right):
    return lax.dot_general(left, right, (((1,), (1,)), ((), ())), preferred_element_type=F32)


def dot_00(left, right):
    return lax.dot_general(left, right, (((0,), (0,)), ((), ())), preferred_element_type=F32)


def hop_exists(way, hop, chunk):
    return hop <= 3 or (hop == 4 and (chunk < CH // 2) == (way == 0))


def kernel(
    x_ref, enc_ref, gain_ref, wq_ref, wk_ref, wv_ref, wo_ref, rows_ref, clen_ref, slen_ref, cost_ref,
    loss_ref, gdec_ref, genc_ref, rad_ref,
    xg, wqf, wof, kvs, kvr, kvo, kvf, dks, dkr, dko, zt, ct, lt, ens, enr, rso, rsr, own,
    xss, xsr, wxs, wxr, wys, wyr, wss, wsr, k1s, k1r, k2s, k2r, d1s, d1r, d2s, d2r,
    zss, zsr, css, csr, lss, lsr, ess, esr, rss, rsrs,
):
    s, c, z = lax.axis_index("source"), lax.axis_index("cand"), lax.axis_index("tensor")
    core, xx, yl = lax.rem(s, 2), c // 2, lax.rem(c, 2)
    sgn = 1 - 2 * core
    tgt, wide = x_ref.shape
    width = wide * N
    cols = wq_ref.shape[1]
    srcs = enc_ref.shape[0]
    pad = kvf.shape[0]
    group = srcs // N
    gpad = pad // N

    def up(i, k):
        return lax.rem(i + k + N, N)

    def remote(src, dst, ssem, rsem, dev):
        return pltpu.make_async_remote_copy(
            src_ref=src, dst_ref=dst, send_sem=ssem, recv_sem=rsem, device_id=dev, device_id_type=MESH
        )

    y_to = {"source": up(s, 2 * yl * (1 - core) - 2 * (1 - yl) * core), "cand": c + 1 - 2 * yl}
    y_from = {"source": up(s, 2 * yl * core - 2 * (1 - yl) * (1 - core)), "cand": c + 1 - 2 * yl}

    barrier = pltpu.get_barrier_semaphore()
    for k in range(1, N):
        pl.semaphore_signal(barrier, inc=1, device_id={"tensor": up(z, k)}, device_id_type=MESH)
        pl.semaphore_signal(barrier, inc=1, device_id={"cand": up(c, k)}, device_id_type=MESH)
        pl.semaphore_signal(barrier, inc=1, device_id={"source": up(s, k)}, device_id_type=MESH)
    pl.semaphore_signal(barrier, inc=1, device_id=y_from, device_id_type=MESH)
    pl.semaphore_wait(barrier, 3 * (N - 1) + 1)

    started = []

    def go(copy):
        copy.start()
        started.append(copy)

    step = tgt // CH

    def x_copy(way, hop, chunk):
        to = 1 if way == 0 else -1
        block = up(z, -to * (hop - 1))
        part = pl.ds(chunk * step, step)
        src = x_ref.at[part] if hop == 1 else xg.at[block, part]
        return remote(src, xg.at[block, part], xss.at[way, hop - 1, chunk], xsr.at[way, hop - 1, chunk], {"tensor": up(z, to)})

    def x_round(hop):
        for chunk in range(CH):
            for way in range(2):
                if hop_exists(way, hop, chunk):
                    x_copy(way, hop, chunk).wait_recv()
                    if hop_exists(way, hop + 1, chunk):
                        go(x_copy(way, hop + 1, chunk))

    hq, ho = wq_ref.shape[0] // 2, wo_ref.shape[0] // 2
    half = (pl.ds(pl.multiple_of(core * hq, hq), hq), pl.ds(pl.multiple_of(core * ho, ho), ho))
    full = (wqf, wof)
    mine = (wq_ref, wo_ref)

    def piece(dx, dy):
        return lax.rem(xx + dx + XS, XS) * 2 + (yl if dy == 0 else 1 - yl)

    def x_dev(to):
        return {"cand": lax.rem(xx + to + XS, XS) * 2 + yl}

    def w_own(m, i):
        return remote(mine[m].at[half[m]], full[m].at[c, half[m]], wxs.at[m, i], wxr.at[m, i], x_dev(1 - 2 * i))

    def w_relay(m):
        there = full[m].at[piece(-sgn, 0), half[m]]
        return remote(there, there, wxs.at[m, 2], wxr.at[m, 2], x_dev(sgn))

    def w_x_wait(m, i):
        remote(mine[m].at[half[m]], full[m].at[c, half[m]], wxs.at[m, i], wxr.at[m, i], x_dev(1)).wait_recv()

    hops = (0, -sgn, sgn, 2)

    def w_y(m, i):
        dst = full[m].at[piece(hops[i], 0), half[m]]
        src = mine[m].at[half[m]] if i == 0 else dst
        return remote(src, dst, wys.at[m, i], wyr.at[m, i], y_to)

    def w_sib(m, i):
        there = full[m].at[piece(hops[i % 4], i // 4), half[m]]
        return remote(there, there, wss.at[m, i - 1], wsr.at[m, i - 1], {"source": s + sgn})

    def w_first(m):
        w_x_wait(m, core)
        go(w_relay(m))
        go(w_y(m, 1))
        go(w_sib(m, 1))
        w_x_wait(m, 1 - core)
        go(w_y(m, 2))
        go(w_sib(m, 2))
        w_y(m, 0).wait_recv()
        go(w_sib(m, 4))

    def w_second(m):
        w_relay(m).wait_recv()
        go(w_y(m, 3))
        go(w_sib(m, 3))
        for i in (1, 2):
            w_y(m, i).wait_recv()
            go(w_sib(m, 4 + i))

    def w_third(m):
        w_y(m, 3).wait_recv()
        go(w_sib(m, 7))

    def w_last(m):
        for i in range(1, N):
            w_sib(m, i).wait_recv()

    for chunk in range(CH):
        for way in range(2):
            go(x_copy(way, 1, chunk))
    for i in range(2):
        go(w_own(0, i))
    go(w_y(0, 0))

    row = lax.broadcasted_iota(jnp.int32, (pad, srcs), 0)
    col = lax.broadcasted_iota(jnp.int32, (pad, srcs), 1)
    spot = lax.rem(row, gpad)
    spread = jnp.where((spot < group) & (row // gpad * group + spot == col), 1.0, 0.0).astype(BF)
    enc = dot(spread, enc_ref[...]).astype(BF)
    k_part = dot(enc, wk_ref[...])
    v_part = dot(enc, wv_ref[...])

    def put_blocks(dst, left, right):
        for g in range(4):
            src = (left if g < 2 else right)[:, (g % 2) * 128 : (g % 2) * 128 + 128].astype(BF)
            for r in range(2):
                dst[g * 2 + r] = src[r * (pad // 2) : (r + 1) * (pad // 2)]

    def cand_all(send_of, dst, ssem, rsem, k):
        return remote(send_of(up(c, k)), dst.at[c], ssem.at[k], rsem.at[k], {"cand": up(c, k)})

    put_blocks(kvs, k_part, v_part)

    def kv1(k):
        return cand_all(lambda i: kvs.at[i], kvr, k1s, k1r, k)

    def kv2(k):
        return cand_all(lambda i: kvo.at[c], kvo, k2s, k2r, k)

    for k in range(1, N):
        go(kv1(k))
    for i in range(2):
        go(w_own(1, i))
    go(w_y(1, 0))

    xg[z] = x_ref[...]
    wqf[c] = wq_ref[...]
    wof[c] = wo_ref[...]

    x_round(1)
    w_first(0)
    x_round(2)
    kvr[c] = kvs[c]
    for k in range(1, N):
        kv1(k).wait_recv()
    total = kvr[0].astype(F32)
    for i in range(1, N):
        total = total + kvr[i].astype(F32)
    kvo[c] = total.astype(BF)
    for k in range(1, N):
        go(kv2(k))
    w_second(0)
    w_first(1)
    x_round(3)
    w_third(0)
    w_second(1)
    x_round(4)
    w_third(1)

    for k in range(1, N):
        kv2(k).wait_recv()
    for g in range(4):
        for r in range(2):
            kvf[r * (pad // 2) : (r + 1) * (pad // 2), g * 128 : (g + 1) * 128] = kvo[g * 2 + r]

    w_last(0)

    def q_step(b, carry):
        acc, squares = carry
        block = xg[b].astype(F32)
        gained = (block * gain_ref[:, pl.ds(pl.multiple_of(b * wide, wide), wide)]).astype(BF)
        return acc + dot(gained, wqf[b]), squares + jnp.sum(block * block, axis=1, keepdims=True)

    q_raw, squares = lax.fori_loop(0, N, q_step, (jnp.zeros((tgt, cols), F32), jnp.zeros((tgt, 1), F32)))
    mean = squares / width + 1e-06
    inv_rms = lax.rsqrt(mean)
    query = (q_raw * inv_rms).astype(BF)

    w_last(1)

    def r_step(b, acc):
        return acc + dot_tt(rows_ref[:, pl.ds(pl.multiple_of(b * wide, wide), wide)], wof[b])

    back = lax.fori_loop(0, N, r_step, jnp.zeros((tgt, cols), F32))
    back_b = back.astype(BF)

    length = jnp.full((tgt, 1), clen_ref[0, 0], jnp.int32)
    inside = (lax.broadcasted_iota(jnp.int32, (tgt, 1), 0) < length).astype(F32)
    factor = inside / jnp.sqrt(width * length.astype(F32))
    place = lax.broadcasted_iota(jnp.int32, (1, pad), 1)
    spot = lax.rem(place, gpad)
    real = (spot < group) & (place // gpad * group + spot < jnp.full((1, pad), slen_ref[0], jnp.int32))
    key_mask = real.astype(F32)
    scale = HEAD_DIM ** (-0.5)
    scaled_back = (back * factor).astype(BF)

    x_part = x_ref[...].astype(F32)
    rows_part = rows_ref[:, pl.ds(pl.multiple_of(z * wide, wide), wide)].astype(F32)
    dots = jnp.sum(x_part * rows_part, axis=1, keepdims=True)
    d_query, d_key, d_value = [], [], []
    for h in range(cols // HEAD_DIM):
        at = slice(h * HEAD_DIM, (h + 1) * HEAD_DIM)
        keys = kvf[:, at]
        values = kvf[:, cols + h * HEAD_DIM : cols + (h + 1) * HEAD_DIM]
        expo = jnp.exp(dot_tt(query[:, at], keys) * scale) * key_mask
        probs = expo / jnp.sum(expo, axis=1, keepdims=True)
        reach = dot_tt(back_b[:, at], values)
        along = jnp.sum(probs * reach, axis=1, keepdims=True)
        dots = dots + along
        d_logits = (probs * (reach - along) * (scale * factor)).astype(BF)
        d_query.append(dot(d_logits, keys))
        d_key.append(dot_00(d_logits, query[:, at]))
        d_value.append(dot_00(probs.astype(BF), scaled_back[:, at]))
    d_query = jnp.concatenate(d_query, axis=1)
    put_blocks(dks, jnp.concatenate(d_key, axis=1), jnp.concatenate(d_value, axis=1))

    eye = lax.broadcasted_iota(jnp.int32, (tgt, tgt), 0) == lax.broadcasted_iota(jnp.int32, (tgt, tgt), 1)
    inner_part = jnp.sum(
        jnp.where(eye, jnp.sum(d_query * q_raw, axis=1, keepdims=True), 0.0), axis=0, keepdims=True
    )
    score_part = jnp.sum(dots * factor, axis=0, keepdims=True)
    line = lax.broadcasted_iota(jnp.int32, (8, 128), 0)
    zt[z] = jnp.where(line == 0, score_part, jnp.where(line == 1, inner_part, 0.0))

    def z_tile(k):
        return remote(zt.at[z], zt.at[z], zss.at[k], zsr.at[k], {"tensor": up(z, k)})

    def c_tile(k):
        return remote(ct.at[c], ct.at[c], css.at[k], csr.at[k], {"cand": up(c, k)})

    def l_tile(k):
        return remote(lt.at[s], lt.at[s], lss.at[k], lsr.at[k], {"source": up(s, k)})

    def dk1(k):
        return cand_all(lambda i: dks.at[i], dkr, d1s, d1r, k)

    def dk2(k):
        return cand_all(lambda i: dko.at[c], dko, d2s, d2r, k)

    def en(k):
        return remote(ens.at[up(z, k)], enr.at[z], ess.at[k], esr.at[k], {"tensor": up(z, k)})

    for k in range(1, N):
        go(z_tile(k))
    for k in range(1, N):
        go(dk1(k))

    dq = d_query.astype(BF)

    def term(dest):
        return dot_tt(dq, wqf[dest])

    def rs_copy(way, hop, chunk):
        part = pl.ds(chunk * step, step)
        return remote(
            rso.at[way, hop - 1, part], rsr.at[way, hop - 1, part],
            rss.at[way, hop - 1, chunk], rsrs.at[way, hop - 1, chunk], {"tensor": up(z, 1 if way == 0 else -1)},
        )

    def rs_round(hop):
        for way in range(2):
            own[way] = term(up(z, hop if way == 0 else -hop))
        fresh = [(w, ch) for w in range(2) for ch in range(CH) if not hop_exists(w, hop + 1, ch)]
        late = [(w, ch) for ch in range(CH) for w in range(2) if hop_exists(w, hop + 1, ch)]
        for way, chunk in fresh + late:
            if not hop_exists(way, hop, chunk):
                continue
            part = pl.ds(chunk * step, step)
            value = own[way, part]
            if hop_exists(way, hop + 1, chunk):
                rs_copy(way, hop + 1, chunk).wait_recv()
                value = value + rsr[way, hop, part].astype(F32)
            rso[way, hop - 1, part] = value.astype(BF)
            go(rs_copy(way, hop, chunk))

    rs_round(4)

    for k in range(1, N):
        z_tile(k).wait_recv()
    sums = zt[0]
    for i in range(1, N):
        sums = sums + zt[i]
    weight = jnp.exp(sums[0:1])
    inner = sums[1:2]
    risk = jnp.full((1, 128), cost_ref[0, 0], jnp.int32).astype(F32) / 100.0
    ct[c] = jnp.where(line == 0, weight, jnp.where(line == 1, risk, 0.0))
    for k in range(1, N):
        go(c_tile(k))

    rs_round(3)

    for k in range(1, N):
        c_tile(k).wait_recv()
    total_w, total_wr = ct[0, 0:1], ct[0, 0:1] * ct[0, 1:2]
    for i in range(1, N):
        total_w = total_w + ct[i, 0:1]
        total_wr = total_wr + ct[i, 0:1] * ct[i, 1:2]
    expected = total_wr / total_w
    lt[s] = jnp.broadcast_to(expected, (8, 128))
    for k in range(1, N):
        go(l_tile(k))
    dkr[c] = dks[c]
    for k in range(1, N):
        dk1(k).wait_recv()
    total = jnp.zeros(dkr.shape[1:], F32)
    for i in range(N):
        share = ct[i, 0:1] / total_w * (ct[i, 1:2] - expected) / N
        total = total + share * dkr[i].astype(F32)
    dko[c] = total.astype(BF)
    for k in range(1, N):
        go(dk2(k))

    rs_round(2)

    for k in range(1, N):
        dk2(k).wait_recv()
    sides = []
    for g in range(4):
        sides.append(jnp.concatenate([dko[g * 2], dko[g * 2 + 1]], axis=0))
    enc_term = dot_tt(jnp.concatenate(sides[:2], axis=1), wk_ref[...])
    enc_term = enc_term + dot_tt(jnp.concatenate(sides[2:], axis=1), wv_ref[...])
    for i in range(N):
        ens[i] = enc_term[i * gpad : (i + 1) * gpad].astype(BF)
    for k in range(1, N):
        go(en(k))

    rs_round(1)

    enr[z] = ens[z]
    for k in range(1, N):
        en(k).wait_recv()
    total = enr[0].astype(F32)
    for i in range(1, N):
        total = total + enr[i].astype(F32)
    genc_ref[...] = total[:group]

    for k in range(1, N):
        l_tile(k).wait_recv()
    loss = lt[0, 0:1]
    for i in range(1, N):
        loss = loss + lt[i, 0:1]
    loss_ref[...] = loss / N

    share = weight / total_w * (risk - expected) / N
    rad_ref[...] = share * inner / jnp.sqrt(jnp.full((1, 128), width, F32))
    share_col = share[:, 0:1]
    inner_col = jnp.sum(jnp.where(eye, inner, 0.0), axis=1, keepdims=True)
    own[0] = term(z)
    for chunk in range(CH):
        for way in range(2):
            rs_copy(way, 1, chunk).wait_recv()
    normed_grad = own[0] + rsr[0, 0].astype(F32) + rsr[1, 0].astype(F32)
    gain_part = gain_ref[:, pl.ds(pl.multiple_of(z * wide, wide), wide)]
    gdec_ref[...] = share_col * (
        factor * rows_part
        + inv_rms * gain_part * normed_grad
        - x_part * (inv_rms * inv_rms * inv_rms * inner_col / width)
    )
    for copy in started:
        copy.wait_send()


def local(
    dec_states, enc_states, norm_gain, w_query, w_key, w_value, w_out, target_rows, cand_lengths, src_lengths, costs
):
    x = dec_states[0, 0]
    enc = enc_states[0]
    tgt, wide = x.shape
    srcs = enc.shape[0]
    depth, cols = w_query.shape
    group = srcs // N
    gpad = -(-group // 16) * 16
    pad = gpad * N
    vmem = pl.BlockSpec(memory_space=pltpu.VMEM)
    smem = pl.BlockSpec(memory_space=pltpu.SMEM)
    dma = pltpu.SemaphoreType.DMA
    block = (N, pad // 2, 128)
    loss, grad_dec, grad_enc, radial = pl.pallas_call(
        kernel,
        out_shape=(
            jax.ShapeDtypeStruct((1, 128), F32),
            jax.ShapeDtypeStruct((tgt, wide), F32),
            jax.ShapeDtypeStruct((group, depth), F32),
            jax.ShapeDtypeStruct((1, tgt), F32),
        ),
        in_specs=[vmem] * 8 + [smem] * 3,
        out_specs=(vmem,) * 4,
        scratch_shapes=[
            pltpu.VMEM((N, tgt, wide), BF),
            pltpu.VMEM((N, depth, cols), BF),
            pltpu.VMEM((N, cols, depth), BF),
            pltpu.VMEM(block, BF),
            pltpu.VMEM(block, BF),
            pltpu.VMEM(block, BF),
            pltpu.VMEM((pad, 2 * cols), BF),
            pltpu.VMEM(block, BF),
            pltpu.VMEM(block, BF),
            pltpu.VMEM(block, BF),
            pltpu.VMEM((N, 8, 128), F32),
            pltpu.VMEM((N, 8, 128), F32),
            pltpu.VMEM((N, 8, 128), F32),
            pltpu.VMEM((N, gpad, depth), BF),
            pltpu.VMEM((N, gpad, depth), BF),
            pltpu.VMEM((2, 4, tgt, wide), BF),
            pltpu.VMEM((2, 4, tgt, wide), BF),
            pltpu.VMEM((2, tgt, wide), F32),
            dma((2, 4, CH)), dma((2, 4, CH)),
            dma((2, 3)), dma((2, 3)),
            dma((2, 4)), dma((2, 4)),
            dma((2, 7)), dma((2, 7)),
        ]
        + [dma((N,))] * 16
        + [dma((2, 4, CH)), dma((2, 4, CH))],
        compiler_params=pltpu.CompilerParams(
            collective_id=0, has_side_effects=True, vmem_limit_bytes=48 * 1024 * 1024
        ),
    )(
        x, enc, norm_gain.reshape(1, -1), w_query, w_key, w_value, w_out, target_rows[0, 0],
        cand_lengths, src_lengths, costs,
    )
    return loss[0, 0], grad_dec[None, None], grad_enc[None], radial[None]


def solution(mesh):
    placed = (
        P("source", "cand", None, "tensor"),
        P("source", None, "cand"),
        P(),
        P("cand", "tensor"),
        P("cand", "tensor"),
        P("cand", "tensor"),
        P("tensor", "cand"),
        P("source", "cand", None, None),
        P("source", "cand"),
        P("source"),
        P("source", "cand"),
    )
    return jax.shard_map(
        local,
        mesh=mesh,
        in_specs=placed,
        out_specs=(
            P(),
            P("source", "cand", None, "tensor"),
            P("source", "tensor", "cand"),
            P("source", "cand", None),
        ),
        check_vma=False,
    )
```

time: 556 us -> 76.2 us (0.14)
  the two profiles are of different devices: /device:TPU:6 before, /device:TPU:8 now
where the time goes in v1:
time: 76.2 us; the launch traced here: 75.7 us
  Pallas kernels  62.6 us (82%)
  local copies, waits for them, and re-layouts  9.38 us (12%)
  between operations  3.77 us (5%)
    pallas_call x1, Pallas kernels, local(): pl.pallas_call(kernel, out_shape=(jax.ShapeDtypeStruct((1, 128), F32), ja...  62.6 us
    unnamed x19, local copies, waits for them, and re-layouts  9.38 us

profile of v1, /device:TPU:8, one launch (start us, length us, event | category | flops | bytes accessed | tf_op | source)
XLA Modules:
  0.0 75.7 jit_solution(1694111277088690124)
XLA Ops:
  2.6 0.0 copy-start
  2.6 1.2 %copy-done = bf16[1,1,128,4096]{3,2,1,0:T(8,128)(2,1)S(1)} copy-done((bf16[1,1,128,4096]{3,2,1,0:T(8,128)(2,1)S(1)}, bf16[1,1,128,4096]{3,2,1,0:T(8,128)(2,1)}, u32[]{:S(2)}) %copy-start) | copy-done | bytes 1048600
  3.8 0.0 copy-start.1
  3.8 0.9 %copy-done.1 = bf16[512,256]{1,0:T(8,128)(2,1)S(1)} copy-done((bf16[512,256]{1,0:T(8,128)(2,1)S(1)}, bf16[512,256]{1,0:T(8,128)(2,1)}, u32[]{:S(2)}) %copy-start.1) | copy-done | bytes 262168
  4.7 0.0 copy-start.2
  4.7 0.9 %copy-done.2 = bf16[512,256]{1,0:T(8,128)(2,1)S(1)} copy-done((bf16[512,256]{1,0:T(8,128)(2,1)S(1)}, bf16[512,256]{1,0:T(8,128)(2,1)}, u32[]{:S(2)}) %copy-start.2) | copy-done | bytes 262168
  5.7 0.0 copy-start.3
  5.7 0.9 %copy-done.3 = bf16[512,256]{1,0:T(8,128)(2,1)S(1)} copy-done((bf16[512,256]{1,0:T(8,128)(2,1)S(1)}, bf16[512,256]{1,0:T(8,128)(2,1)}, u32[]{:S(2)}) %copy-start.3) | copy-done | bytes 262168
  6.6 0.0 copy-start.4
  6.7 0.9 %copy-done.4 = bf16[256,512]{1,0:T(8,128)(2,1)S(1)} copy-done((bf16[256,512]{1,0:T(8,128)(2,1)S(1)}, bf16[256,512]{1,0:T(8,128)(2,1)}, u32[]{:S(2)}) %copy-start.4) | copy-done | bytes 262168
  7.6 0.0 copy-start.5
  7.6 0.9 %copy-done.5 = bf16[1,1,128,512]{3,2,1,0:T(8,128)(2,1)S(1)} copy-done((bf16[1,1,128,512]{3,2,1,0:T(8,128)(2,1)S(1)}, bf16[1,1,128,512]{3,2,1,0:T(8,128)(2,1)}, u32[]{:S(2)}) %copy-start.5) | copy-done | bytes 131096
  8.5 0.0 copy-start.6
  8.5 0.9 %copy-done.6 = bf16[1,96,512]{2,1,0:T(8,128)(2,1)S(1)} copy-done((bf16[1,96,512]{2,1,0:T(8,128)(2,1)S(1)}, bf16[1,96,512]{2,1,0:T(8,128)(2,1)}, u32[]{:S(2)}) %copy-start.6) | copy-done | bytes 98328
  9.4 0.0 copy-start.7
  9.4 0.7 copy-done.7
  10.1 62.6 %shard_map.138 = (f32[1,128]{1,0:T(1,128)S(1)}, f32[128,512]{1,0:T(8,128)S(1)}, f32[12,512]{1,0:T(8,128)S(1)}, f32[1,128]{1,0:T(1,128)S(1)}) custom-call(bf16[128,512]{1,0:T(8,128)(2,1)S(1)} %bitcast.11, bf16[96,512]{1,0:T(8,128)(2,1)S(1)} %bitcast.12, f32[1,4096]{1,0:T(1,128)S(1)} %bitcast.14, bf16[512,256]{1,0:T(8,128)(2,1)S(1)} %copy-done.1, ...), custom_call_target="tpu_custom_call" | custom-call | tf_op jit(solution)/shard_map/pallas_call | solution.py:432
  72.7 0.6 copy.15
  73.4 0.7 copy.23
  74.1 0.5 copy.24
Async XLA Ops:
  2.6 1.2 %copy-start = (bf16[1,1,128,4096]{3,2,1,0:T(8,128)(2,1)S(1)}, bf16[1,1,128,4096]{3,2,1,0:T(8,128)(2,1)}, u32[]{:S(2)}) copy-start(bf16[1,1,128,4096]{3,2,1,0:T(8,128)(2,1)} %param.18) | copy-start | bytes 3145732
  3.8 0.9 %copy-start.1 = (bf16[512,256]{1,0:T(8,128)(2,1)S(1)}, bf16[512,256]{1,0:T(8,128)(2,1)}, u32[]{:S(2)}) copy-start(bf16[512,256]{1,0:T(8,128)(2,1)} %wq_ref.1) | copy-start | bytes 786436
  4.7 0.9 %copy-start.2 = (bf16[512,256]{1,0:T(8,128)(2,1)S(1)}, bf16[512,256]{1,0:T(8,128)(2,1)}, u32[]{:S(2)}) copy-start(bf16[512,256]{1,0:T(8,128)(2,1)} %wk_ref.1) | copy-start | bytes 786436
  5.7 0.9 %copy-start.3 = (bf16[512,256]{1,0:T(8,128)(2,1)S(1)}, bf16[512,256]{1,0:T(8,128)(2,1)}, u32[]{:S(2)}) copy-start(bf16[512,256]{1,0:T(8,128)(2,1)} %wv_ref.1) | copy-start | bytes 786436
  6.6 0.9 %copy-start.4 = (bf16[256,512]{1,0:T(8,128)(2,1)S(1)}, bf16[256,512]{1,0:T(8,128)(2,1)}, u32[]{:S(2)}) copy-start(bf16[256,512]{1,0:T(8,128)(2,1)} %wo_ref.1) | copy-start | bytes 786436
  7.6 0.9 %copy-start.5 = (bf16[1,1,128,512]{3,2,1,0:T(8,128)(2,1)S(1)}, bf16[1,1,128,512]{3,2,1,0:T(8,128)(2,1)}, u32[]{:S(2)}) copy-start(bf16[1,1,128,512]{3,2,1,0:T(8,128)(2,1)} %param.11) | copy-start | bytes 393220
  8.5 0.9 %copy-start.6 = (bf16[1,96,512]{2,1,0:T(8,128)(2,1)S(1)}, bf16[1,96,512]{2,1,0:T(8,128)(2,1)}, u32[]{:S(2)}) copy-start(bf16[1,96,512]{2,1,0:T(8,128)(2,1)} %param.12) | copy-start | bytes 294916
  9.4 0.7 copy-start.7

commit v2 on v1

--- a/solution.py
+++ b/solution.py
@@ -8,7 +8,7 @@
 HEAD_DIM = 64
 N = 8
 XS = 4
-CH = 4
+CH = 2
 MESH = pl.DeviceIdType.MESH
 BF = jnp.bfloat16
 F32 = jnp.float32
@@ -31,18 +31,18 @@
 
 
 def kernel(
-    x_ref, enc_ref, gain_ref, wq_ref, wk_ref, wv_ref, wo_ref, rows_ref, clen_ref, slen_ref, cost_ref,
+    x_in, enc_in, gain_in, wq_in, wk_in, wv_in, wo_in, rows_in, clen_ref, slen_ref, cost_ref,
     loss_ref, gdec_ref, genc_ref, rad_ref,
-    xg, wqf, wof, kvs, kvr, kvo, kvf, dks, dkr, dko, zt, ct, lt, ens, enr, rso, rsr, own,
+    enc_ref, gain_ref, wk_ref, wv_ref, rows_ref, loads, xn, xg, wqf, wof, kvs, kvr, kvo, kvf, dks, dkr, dko, zt, ct, lt, ens, enr, rso, rsr, own,
     xss, xsr, wxs, wxr, wys, wyr, wss, wsr, k1s, k1r, k2s, k2r, d1s, d1r, d2s, d2r,
     zss, zsr, css, csr, lss, lsr, ess, esr, rss, rsrs,
 ):
     s, c, z = lax.axis_index("source"), lax.axis_index("cand"), lax.axis_index("tensor")
     core, xx, yl = lax.rem(s, 2), c // 2, lax.rem(c, 2)
     sgn = 1 - 2 * core
-    tgt, wide = x_ref.shape
+    tgt, wide = x_in.shape
     width = wide * N
-    cols = wq_ref.shape[1]
+    cols = wq_in.shape[1]
     srcs = enc_ref.shape[0]
     pad = kvf.shape[0]
     group = srcs // N
@@ -58,6 +58,16 @@
 
     y_to = {"source": up(s, 2 * yl * (1 - core) - 2 * (1 - yl) * core), "cand": c + 1 - 2 * yl}
     y_from = {"source": up(s, 2 * yl * core - 2 * (1 - yl) * (1 - core)), "cand": c + 1 - 2 * yl}
+
+    x_own, wq_own, wo_own = xg.at[z], wqf.at[c], wof.at[c]
+    into = (x_own, wq_own, enc_ref, wk_ref, wv_ref, wo_own, rows_ref, gain_ref)
+    local_copies = [
+        pltpu.make_async_copy(src, dst, loads.at[i])
+        for i, (src, dst) in enumerate(zip((x_in, wq_in, enc_in, wk_in, wv_in, wo_in, rows_in, gain_in), into))
+    ]
+    for copy in local_copies:
+        copy.start()
+    x_load, wq_load, enc_load, wk_load, wv_load, wo_load, rows_load, gain_load = local_copies
 
     barrier = pltpu.get_barrier_semaphore()
     for k in range(1, N):
@@ -79,8 +89,7 @@
         to = 1 if way == 0 else -1
         block = up(z, -to * (hop - 1))
         part = pl.ds(chunk * step, step)
-        src = x_ref.at[part] if hop == 1 else xg.at[block, part]
-        return remote(src, xg.at[block, part], xss.at[way, hop - 1, chunk], xsr.at[way, hop - 1, chunk], {"tensor": up(z, to)})
+        return remote(xg.at[block, part], xg.at[block, part], xss.at[way, hop - 1, chunk], xsr.at[way, hop - 1, chunk], {"tensor": up(z, to)})
 
     def x_round(hop):
         for chunk in range(CH):
@@ -90,10 +99,9 @@
                     if hop_exists(way, hop + 1, chunk):
                         go(x_copy(way, hop + 1, chunk))
 
-    hq, ho = wq_ref.shape[0] // 2, wo_ref.shape[0] // 2
+    hq, ho = wq_in.shape[0] // 2, wo_in.shape[0] // 2
     half = (pl.ds(pl.multiple_of(core * hq, hq), hq), pl.ds(pl.multiple_of(core * ho, ho), ho))
     full = (wqf, wof)
-    mine = (wq_ref, wo_ref)
 
     def piece(dx, dy):
         return lax.rem(xx + dx + XS, XS) * 2 + (yl if dy == 0 else 1 - yl)
@@ -102,27 +110,28 @@
         return {"cand": lax.rem(xx + to + XS, XS) * 2 + yl}
 
     def w_own(m, i):
-        return remote(mine[m].at[half[m]], full[m].at[c, half[m]], wxs.at[m, i], wxr.at[m, i], x_dev(1 - 2 * i))
+        there = full[m].at[c, half[m]]
+        return remote(there, there, wxs.at[m, i], wxr.at[m, i], x_dev(1 - 2 * i))
 
     def w_relay(m):
         there = full[m].at[piece(-sgn, 0), half[m]]
         return remote(there, there, wxs.at[m, 2], wxr.at[m, 2], x_dev(sgn))
 
     def w_x_wait(m, i):
-        remote(mine[m].at[half[m]], full[m].at[c, half[m]], wxs.at[m, i], wxr.at[m, i], x_dev(1)).wait_recv()
+        there = full[m].at[c, half[m]]
+        remote(there, there, wxs.at[m, i], wxr.at[m, i], x_dev(1)).wait_recv()
 
     hops = (0, -sgn, sgn, 2)
 
     def w_y(m, i):
-        dst = full[m].at[piece(hops[i], 0), half[m]]
-        src = mine[m].at[half[m]] if i == 0 else dst
-        return remote(src, dst, wys.at[m, i], wyr.at[m, i], y_to)
+        there = full[m].at[piece(hops[i], 0), half[m]]
+        return remote(there, there, wys.at[m, i], wyr.at[m, i], y_to)
 
     def w_sib(m, i):
         there = full[m].at[piece(hops[i % 4], i // 4), half[m]]
         return remote(there, there, wss.at[m, i - 1], wsr.at[m, i - 1], {"source": s + sgn})
 
-    def w_first(m):
+    def w_near(m):
         w_x_wait(m, core)
         go(w_relay(m))
         go(w_y(m, 1))
@@ -130,36 +139,48 @@
         w_x_wait(m, 1 - core)
         go(w_y(m, 2))
         go(w_sib(m, 2))
+
+    def w_across(m):
         w_y(m, 0).wait_recv()
         go(w_sib(m, 4))
 
-    def w_second(m):
+    def w_far(m):
         w_relay(m).wait_recv()
         go(w_y(m, 3))
         go(w_sib(m, 3))
+
+    def w_corner(m):
         for i in (1, 2):
             w_y(m, i).wait_recv()
             go(w_sib(m, 4 + i))
 
-    def w_third(m):
+    def w_end(m):
         w_y(m, 3).wait_recv()
         go(w_sib(m, 7))
 
-    def w_last(m):
-        for i in range(1, N):
-            w_sib(m, i).wait_recv()
-
+    def w_got(m, i):
+        w_sib(m, i).wait_recv()
+
+    x_load.wait()
     for chunk in range(CH):
         for way in range(2):
             go(x_copy(way, 1, chunk))
+    wq_load.wait()
     for i in range(2):
         go(w_own(0, i))
     go(w_y(0, 0))
+    wo_load.wait()
+    for i in range(2):
+        go(w_own(1, i))
+    go(w_y(1, 0))
 
     row = lax.broadcasted_iota(jnp.int32, (pad, srcs), 0)
     col = lax.broadcasted_iota(jnp.int32, (pad, srcs), 1)
     spot = lax.rem(row, gpad)
     spread = jnp.where((spot < group) & (row // gpad * group + spot == col), 1.0, 0.0).astype(BF)
+    enc_load.wait()
+    wk_load.wait()
+    wv_load.wait()
     enc = dot(spread, enc_ref[...]).astype(BF)
     k_part = dot(enc, wk_ref[...])
     v_part = dot(enc, wv_ref[...])
@@ -183,17 +204,26 @@
 
     for k in range(1, N):
         go(kv1(k))
-    for i in range(2):
-        go(w_own(1, i))
-    go(w_y(1, 0))
-
-    xg[z] = x_ref[...]
-    wqf[c] = wq_ref[...]
-    wof[c] = wo_ref[...]
-
+    gain_load.wait()
+    rows_load.wait()
+
+    def gained(b):
+        block = xg[b].astype(F32)
+        xn[:, pl.ds(pl.multiple_of(b * wide, wide), wide)] = (
+            block * gain_ref[:, pl.ds(pl.multiple_of(b * wide, wide), wide)]
+        ).astype(BF)
+        return jnp.sum(block * block, axis=1, keepdims=True)
+
+    def r_term(b):
+        return dot_tt(rows_ref[:, pl.ds(pl.multiple_of(b * wide, wide), wide)], wof[b])
+
+    squares = gained(z)
+    back = r_term(c)
+    w_across(0)
     x_round(1)
-    w_first(0)
-    x_round(2)
+    w_near(0)
+    w_across(1)
+    squares = squares + gained(up(z, 1)) + gained(up(z, -1))
     kvr[c] = kvs[c]
     for k in range(1, N):
         kv1(k).wait_recv()
@@ -203,39 +233,43 @@
     kvo[c] = total.astype(BF)
     for k in range(1, N):
         go(kv2(k))
-    w_second(0)
-    w_first(1)
+    x_round(2)
+    w_near(1)
+    w_far(0)
+    squares = squares + gained(up(z, 2)) + gained(up(z, -2))
+    w_corner(0)
+    w_far(1)
     x_round(3)
-    w_third(0)
-    w_second(1)
+    squares = squares + gained(up(z, 3)) + gained(up(z, -3))
+    w_got(1, 4)
+    back = back + r_term(piece(0, 1))
+    w_got(1, 1)
+    w_got(1, 2)
+    back = back + r_term(piece(1, 0)) + r_term(piece(-1, 0))
+    w_corner(1)
+    w_end(0)
     x_round(4)
-    w_third(1)
-
+    squares = squares + gained(up(z, 4))
+    w_got(1, 3)
+    back = back + r_term(piece(2, 0))
     for k in range(1, N):
         kv2(k).wait_recv()
     for g in range(4):
         for r in range(2):
             kvf[r * (pad // 2) : (r + 1) * (pad // 2), g * 128 : (g + 1) * 128] = kvo[g * 2 + r]
-
-    w_last(0)
-
-    def q_step(b, carry):
-        acc, squares = carry
-        block = xg[b].astype(F32)
-        gained = (block * gain_ref[:, pl.ds(pl.multiple_of(b * wide, wide), wide)]).astype(BF)
-        return acc + dot(gained, wqf[b]), squares + jnp.sum(block * block, axis=1, keepdims=True)
-
-    q_raw, squares = lax.fori_loop(0, N, q_step, (jnp.zeros((tgt, cols), F32), jnp.zeros((tgt, 1), F32)))
-    mean = squares / width + 1e-06
-    inv_rms = lax.rsqrt(mean)
+    w_end(1)
+    for i in range(1, N):
+        w_got(0, i)
+    q_raw = jnp.zeros((tgt, cols), F32)
+    for b in range(N):
+        q_raw = q_raw + dot(xn[:, b * wide : (b + 1) * wide], wqf[b])
+    inv_rms = lax.rsqrt(squares / width + 1e-06)
     query = (q_raw * inv_rms).astype(BF)
-
-    w_last(1)
-
-    def r_step(b, acc):
-        return acc + dot_tt(rows_ref[:, pl.ds(pl.multiple_of(b * wide, wide), wide)], wof[b])
-
-    back = lax.fori_loop(0, N, r_step, jnp.zeros((tgt, cols), F32))
+    w_got(1, 5)
+    w_got(1, 6)
+    back = back + r_term(piece(1, 1)) + r_term(piece(-1, 1))
+    w_got(1, 7)
+    back = back + r_term(piece(2, 1))
     back_b = back.astype(BF)
 
     length = jnp.full((tgt, 1), clen_ref[0, 0], jnp.int32)
@@ -248,7 +282,7 @@
     scale = HEAD_DIM ** (-0.5)
     scaled_back = (back * factor).astype(BF)
 
-    x_part = x_ref[...].astype(F32)
+    x_part = xg[z].astype(F32)
     rows_part = rows_ref[:, pl.ds(pl.multiple_of(z * wide, wide), wide)].astype(F32)
     dots = jnp.sum(x_part * rows_part, axis=1, keepdims=True)
     d_query, d_key, d_value = [], [], []
@@ -437,9 +471,16 @@
             jax.ShapeDtypeStruct((group, depth), F32),
             jax.ShapeDtypeStruct((1, tgt), F32),
         ),
-        in_specs=[vmem] * 8 + [smem] * 3,
+        in_specs=[pl.BlockSpec(memory_space=pltpu.HBM)] * 8 + [smem] * 3,
         out_specs=(vmem,) * 4,
         scratch_shapes=[
+            pltpu.VMEM(enc.shape, BF),
+            pltpu.VMEM((1, wide * N), F32),
+            pltpu.VMEM((depth, cols), BF),
+            pltpu.VMEM((depth, cols), BF),
+            pltpu.VMEM((tgt, wide * N), BF),
+            dma((8,)),
+            pltpu.VMEM((tgt, wide * N), BF),
             pltpu.VMEM((N, tgt, wide), BF),
             pltpu.VMEM((N, depth, cols), BF),
             pltpu.VMEM((N, cols, depth), BF),
@@ -466,10 +507,13 @@
         + [dma((N,))] * 16
         + [dma((2, 4, CH)), dma((2, 4, CH))],
         compiler_params=pltpu.CompilerParams(
-            collective_id=0, has_side_effects=True, vmem_limit_bytes=48 * 1024 * 1024
+            collective_id=0, has_side_effects=True, vmem_limit_bytes=40 * 1024 * 1024
         ),
     )(
-        x, enc, norm_gain.reshape(1, -1), w_query, w_key, w_value, w_out, target_rows[0, 0],
+        *(
+            pltpu.with_memory_space_constraint(array, pltpu.HBM)
+            for array in (x, enc, norm_gain.reshape(1, -1), w_query, w_key, w_value, w_out, target_rows[0, 0])
+        ),
         cand_lengths, src_lengths, costs,
     )
     return loss[0, 0], grad_dec[None, None], grad_enc[None], radial[None]

time: 76.2 us -> 64.9 us (0.85)
  local copies, waits for them, and re-layouts: 9.38 us -> 1.85 us
  Pallas kernels: 62.6 us -> 59.1 us
    unnamed x19 -> x3, local copies, waits for them, and re-layouts: 9.38 us -> 1.85 us
    pallas_call x1, Pallas kernels: 62.6 us -> 59.1 us  [local(): pl.pallas_call(kernel, out_shape=(jax.ShapeDtypeStruct((1, 128), F32), ja...]
where the time goes in v2:
time: 64.9 us; the launch traced here: 64.7 us
  Pallas kernels  59.1 us (91%)
  between operations  3.75 us (6%)
  local copies, waits for them, and re-layouts  1.85 us (3%)
    pallas_call x1, Pallas kernels, local(): pl.pallas_call(kernel, out_shape=(jax.ShapeDtypeStruct((1, 128), F32), ja...  59.1 us
    unnamed x3, local copies, waits for them, and re-layouts  1.85 us

profile of v2, /device:TPU:8, one launch (start us, length us, event | category | flops | bytes accessed | tf_op | source)
XLA Modules:
  0.0 64.7 jit_solution(14129903673572463249)
XLA Ops:
  2.6 59.1 %shard_map.138 = (f32[1,128]{1,0:T(1,128)S(1)}, f32[128,512]{1,0:T(8,128)S(1)}, f32[12,512]{1,0:T(8,128)S(1)}, f32[1,128]{1,0:T(1,128)S(1)}) custom-call(bf16[128,512]{1,0:T(8,128)(2,1)} %bitcast.14, bf16[96,512]{1,0:T(8,128)(2,1)} %bitcast.15, f32[1,4096]{1,0:T(1,128)} %bitcast.16, bf16[512,256]{1,0:T(8,128)(2,1)} %wq_in.1, bf16[512,256]{1,0:T(8,128)(2,1)} %wk_in.1, ...), custom_call_target="tpu_custom_call" | custom-call | tf_op jit(solution)/shard_map/pallas_call | solution.py:466
  61.7 0.6 copy.15
  62.4 0.7 %copy.23 = f32[1,1,128,512]{3,2,1,0:T(8,128)} copy(f32[1,1,128,512]{3,2,1,0:T(8,128)S(1)} %bitcast.9) | data formatting | bytes 524288
  63.1 0.5 copy.24

commit v3 on v2

--- a/solution.py
+++ b/solution.py
@@ -8,6 +8,7 @@
 HEAD_DIM = 64
 N = 8
 XS = 4
+WCH = 1
 CH = 2
 MESH = pl.DeviceIdType.MESH
 BF = jnp.bfloat16
@@ -33,8 +34,8 @@
 def kernel(
     x_in, enc_in, gain_in, wq_in, wk_in, wv_in, wo_in, rows_in, clen_ref, slen_ref, cost_ref,
     loss_ref, gdec_ref, genc_ref, rad_ref,
-    enc_ref, gain_ref, wk_ref, wv_ref, rows_ref, loads, xn, xg, wqf, wof, kvs, kvr, kvo, kvf, dks, dkr, dko, zt, ct, lt, ens, enr, rso, rsr, own,
-    xss, xsr, wxs, wxr, wys, wyr, wss, wsr, k1s, k1r, k2s, k2r, d1s, d1r, d2s, d2r,
+    enc_ref, gain_ref, wk_ref, wv_ref, rows_ref, loads, xn, xg, wqf, wof, kvs, kvr, kvo, kvf, dks, dkr, dko, zt, it, ct, lt, ens, enr, rso, rsr, own,
+    its, itr, xss, xsr, wxs, wxr, wys, wyr, wss, wsr, k1s, k1r, k2s, k2r, d1s, d1r, d2s, d2r,
     zss, zsr, css, csr, lss, lsr, ess, esr, rss, rsrs,
 ):
     s, c, z = lax.axis_index("source"), lax.axis_index("cand"), lax.axis_index("tensor")
@@ -78,10 +79,17 @@
     pl.semaphore_wait(barrier, 3 * (N - 1) + 1)
 
     started = []
+    far_z, far_c = (4, 3, 5, 2, 6, 1, 7), (5, 4, 3, 2, 6, 7, 1)
 
     def go(copy):
         copy.start()
         started.append(copy)
+
+    def drain(keep=0):
+        done = started[: len(started) - keep]
+        del started[: len(started) - keep]
+        for copy in done:
+            copy.wait_send()
 
     step = tgt // CH
 
@@ -89,7 +97,8 @@
         to = 1 if way == 0 else -1
         block = up(z, -to * (hop - 1))
         part = pl.ds(chunk * step, step)
-        return remote(xg.at[block, part], xg.at[block, part], xss.at[way, hop - 1, chunk], xsr.at[way, hop - 1, chunk], {"tensor": up(z, to)})
+        src = x_in.at[part] if hop == 1 else xg.at[block, part]
+        return remote(src, xg.at[block, part], xss.at[way, hop - 1, chunk], xsr.at[way, hop - 1, chunk], {"tensor": up(z, to)})
 
     def x_round(hop):
         for chunk in range(CH):
@@ -99,9 +108,15 @@
                     if hop_exists(way, hop + 1, chunk):
                         go(x_copy(way, hop + 1, chunk))
 
-    hq, ho = wq_in.shape[0] // 2, wo_in.shape[0] // 2
-    half = (pl.ds(pl.multiple_of(core * hq, hq), hq), pl.ds(pl.multiple_of(core * ho, ho), ho))
-    full = (wqf, wof)
+    hq, ho = wq_in.shape[0] // (2 * WCH), wo_in.shape[0] // (2 * WCH)
+    mine = [wq_in] * WCH + [wo_in] * WCH
+    full, half = [], []
+    for j in range(WCH):
+        half.append(pl.ds(pl.multiple_of((core * WCH + j) * hq, hq), hq))
+        full.append(wqf)
+    for j in range(WCH):
+        half.append(pl.ds(pl.multiple_of((core * WCH + j) * ho, ho), ho))
+        full.append(wof)
 
     def piece(dx, dy):
         return lax.rem(xx + dx + XS, XS) * 2 + (yl if dy == 0 else 1 - yl)
@@ -110,8 +125,7 @@
         return {"cand": lax.rem(xx + to + XS, XS) * 2 + yl}
 
     def w_own(m, i):
-        there = full[m].at[c, half[m]]
-        return remote(there, there, wxs.at[m, i], wxr.at[m, i], x_dev(1 - 2 * i))
+        return remote(mine[m].at[half[m]], full[m].at[c, half[m]], wxs.at[m, i], wxr.at[m, i], x_dev(1 - 2 * i))
 
     def w_relay(m):
         there = full[m].at[piece(-sgn, 0), half[m]]
@@ -125,7 +139,7 @@
 
     def w_y(m, i):
         there = full[m].at[piece(hops[i], 0), half[m]]
-        return remote(there, there, wys.at[m, i], wyr.at[m, i], y_to)
+        return remote(mine[m].at[half[m]] if i == 0 else there, there, wys.at[m, i], wyr.at[m, i], y_to)
 
     def w_sib(m, i):
         there = full[m].at[piece(hops[i % 4], i // 4), half[m]]
@@ -161,18 +175,18 @@
     def w_got(m, i):
         w_sib(m, i).wait_recv()
 
-    x_load.wait()
+    firsts, seconds = range(WCH), range(WCH, 2 * WCH)
+
+    def w_start(m):
+        for i in range(2):
+            go(w_own(m, i))
+        go(w_y(m, 0))
+
     for chunk in range(CH):
         for way in range(2):
             go(x_copy(way, 1, chunk))
-    wq_load.wait()
-    for i in range(2):
-        go(w_own(0, i))
-    go(w_y(0, 0))
-    wo_load.wait()
-    for i in range(2):
-        go(w_own(1, i))
-    go(w_y(1, 0))
+    for m in range(2 * WCH):
+        w_start(m)
 
     row = lax.broadcasted_iota(jnp.int32, (pad, srcs), 0)
     col = lax.broadcasted_iota(jnp.int32, (pad, srcs), 1)
@@ -202,7 +216,7 @@
     def kv2(k):
         return cand_all(lambda i: kvo.at[c], kvo, k2s, k2r, k)
 
-    for k in range(1, N):
+    for k in far_c:
         go(kv1(k))
     gain_load.wait()
     rows_load.wait()
@@ -217,13 +231,16 @@
     def r_term(b):
         return dot_tt(rows_ref[:, pl.ds(pl.multiple_of(b * wide, wide), wide)], wof[b])
 
+    wq_load.wait()
+    wo_load.wait()
+    x_load.wait()
     squares = gained(z)
-    back = r_term(c)
     w_across(0)
     x_round(1)
     w_near(0)
     w_across(1)
-    squares = squares + gained(up(z, 1)) + gained(up(z, -1))
+    x_round(2)
+    w_near(1)
     kvr[c] = kvs[c]
     for k in range(1, N):
         kv1(k).wait_recv()
@@ -231,33 +248,33 @@
     for i in range(1, N):
         total = total + kvr[i].astype(F32)
     kvo[c] = total.astype(BF)
-    for k in range(1, N):
+    for k in far_c:
         go(kv2(k))
-    x_round(2)
-    w_near(1)
     w_far(0)
-    squares = squares + gained(up(z, 2)) + gained(up(z, -2))
+    x_round(3)
     w_corner(0)
     w_far(1)
-    x_round(3)
+    squares = squares + gained(up(z, 1)) + gained(up(z, -1)) + gained(up(z, 2)) + gained(up(z, -2))
+    back = r_term(c)
+    w_corner(1)
+    for i in (1, 2, 4):
+        w_got(1, i)
+    back = back + r_term(piece(0, 1)) + r_term(piece(1, 0)) + r_term(piece(-1, 0))
+    x_round(4)
     squares = squares + gained(up(z, 3)) + gained(up(z, -3))
-    w_got(1, 4)
-    back = back + r_term(piece(0, 1))
-    w_got(1, 1)
-    w_got(1, 2)
-    back = back + r_term(piece(1, 0)) + r_term(piece(-1, 0))
-    w_corner(1)
     w_end(0)
-    x_round(4)
-    squares = squares + gained(up(z, 4))
     w_got(1, 3)
     back = back + r_term(piece(2, 0))
+    w_got(1, 5)
+    w_got(1, 6)
+    back = back + r_term(piece(1, 1)) + r_term(piece(-1, 1))
+    w_end(1)
+    squares = squares + gained(up(z, 4))
     for k in range(1, N):
         kv2(k).wait_recv()
     for g in range(4):
         for r in range(2):
             kvf[r * (pad // 2) : (r + 1) * (pad // 2), g * 128 : (g + 1) * 128] = kvo[g * 2 + r]
-    w_end(1)
     for i in range(1, N):
         w_got(0, i)
     q_raw = jnp.zeros((tgt, cols), F32)
@@ -265,9 +282,6 @@
         q_raw = q_raw + dot(xn[:, b * wide : (b + 1) * wide], wqf[b])
     inv_rms = lax.rsqrt(squares / width + 1e-06)
     query = (q_raw * inv_rms).astype(BF)
-    w_got(1, 5)
-    w_got(1, 6)
-    back = back + r_term(piece(1, 1)) + r_term(piece(-1, 1))
     w_got(1, 7)
     back = back + r_term(piece(2, 1))
     back_b = back.astype(BF)
@@ -280,35 +294,24 @@
     real = (spot < group) & (place // gpad * group + spot < jnp.full((1, pad), slen_ref[0], jnp.int32))
     key_mask = real.astype(F32)
     scale = HEAD_DIM ** (-0.5)
-    scaled_back = (back * factor).astype(BF)
-
     x_part = xg[z].astype(F32)
     rows_part = rows_ref[:, pl.ds(pl.multiple_of(z * wide, wide), wide)].astype(F32)
     dots = jnp.sum(x_part * rows_part, axis=1, keepdims=True)
-    d_query, d_key, d_value = [], [], []
-    for h in range(cols // HEAD_DIM):
-        at = slice(h * HEAD_DIM, (h + 1) * HEAD_DIM)
-        keys = kvf[:, at]
-        values = kvf[:, cols + h * HEAD_DIM : cols + (h + 1) * HEAD_DIM]
-        expo = jnp.exp(dot_tt(query[:, at], keys) * scale) * key_mask
-        probs = expo / jnp.sum(expo, axis=1, keepdims=True)
-        reach = dot_tt(back_b[:, at], values)
-        along = jnp.sum(probs * reach, axis=1, keepdims=True)
-        dots = dots + along
-        d_logits = (probs * (reach - along) * (scale * factor)).astype(BF)
-        d_query.append(dot(d_logits, keys))
-        d_key.append(dot_00(d_logits, query[:, at]))
-        d_value.append(dot_00(probs.astype(BF), scaled_back[:, at]))
-    d_query = jnp.concatenate(d_query, axis=1)
-    put_blocks(dks, jnp.concatenate(d_key, axis=1), jnp.concatenate(d_value, axis=1))
-
     eye = lax.broadcasted_iota(jnp.int32, (tgt, tgt), 0) == lax.broadcasted_iota(jnp.int32, (tgt, tgt), 1)
-    inner_part = jnp.sum(
-        jnp.where(eye, jnp.sum(d_query * q_raw, axis=1, keepdims=True), 0.0), axis=0, keepdims=True
-    )
+    line = lax.broadcasted_iota(jnp.int32, (8, 128), 0)
+
+    heads = [slice(h * HEAD_DIM, (h + 1) * HEAD_DIM) for h in range(cols // HEAD_DIM)]
+    probs = []
+    for at in heads:
+        expo = jnp.exp(dot_tt(query[:, at], kvf[:, at]) * scale) * key_mask
+        probs.append(expo / jnp.sum(expo, axis=1, keepdims=True))
+    reach, along = [], []
+    for h, at in enumerate(heads):
+        reach.append(dot_tt(back_b[:, at], kvf[:, cols + h * HEAD_DIM : cols + (h + 1) * HEAD_DIM]))
+        along.append(jnp.sum(probs[h] * reach[h], axis=1, keepdims=True))
+        dots = dots + along[h]
     score_part = jnp.sum(dots * factor, axis=0, keepdims=True)
-    line = lax.broadcasted_iota(jnp.int32, (8, 128), 0)
-    zt[z] = jnp.where(line == 0, score_part, jnp.where(line == 1, inner_part, 0.0))
+    zt[z] = jnp.broadcast_to(score_part, (8, 128))
 
     def z_tile(k):
         return remote(zt.at[z], zt.at[z], zss.at[k], zsr.at[k], {"tensor": up(z, k)})
@@ -328,10 +331,17 @@
     def en(k):
         return remote(ens.at[up(z, k)], enr.at[z], ess.at[k], esr.at[k], {"tensor": up(z, k)})
 
-    for k in range(1, N):
+    def i_tile(k):
+        return remote(it.at[z], it.at[z], its.at[k], itr.at[k], {"tensor": up(z, k)})
+
+    for k in far_z:
         go(z_tile(k))
-    for k in range(1, N):
-        go(dk1(k))
+
+    d_logits, d_query = [], []
+    for h, at in enumerate(heads):
+        d_logits.append((probs[h] * (reach[h] - along[h]) * (scale * factor)).astype(BF))
+        d_query.append(dot(d_logits[h], kvf[:, at]))
+    d_query = jnp.concatenate(d_query, axis=1)
 
     dq = d_query.astype(BF)
 
@@ -346,15 +356,16 @@
         )
 
     def rs_round(hop):
-        for way in range(2):
-            own[way] = term(up(z, hop if way == 0 else -hop))
+        own[0] = term(up(z, hop))
+        if hop < 4:
+            own[1] = term(up(z, -hop))
         fresh = [(w, ch) for w in range(2) for ch in range(CH) if not hop_exists(w, hop + 1, ch)]
         late = [(w, ch) for ch in range(CH) for w in range(2) if hop_exists(w, hop + 1, ch)]
         for way, chunk in fresh + late:
             if not hop_exists(way, hop, chunk):
                 continue
             part = pl.ds(chunk * step, step)
-            value = own[way, part]
+            value = own[way if hop < 4 else 0, part]
             if hop_exists(way, hop + 1, chunk):
                 rs_copy(way, hop + 1, chunk).wait_recv()
                 value = value + rsr[way, hop, part].astype(F32)
@@ -363,17 +374,32 @@
 
     rs_round(4)
 
+    scaled_back = (back * factor).astype(BF)
+    d_key, d_value = [], []
+    for h, at in enumerate(heads):
+        d_key.append(dot_00(d_logits[h], query[:, at]))
+        d_value.append(dot_00(probs[h].astype(BF), scaled_back[:, at]))
+    put_blocks(dks, jnp.concatenate(d_key, axis=1), jnp.concatenate(d_value, axis=1))
+    for k in far_c:
+        go(dk1(k))
+    inner_part = jnp.sum(
+        jnp.where(eye, jnp.sum(d_query * q_raw, axis=1, keepdims=True), 0.0), axis=0, keepdims=True
+    )
+    it[z] = jnp.broadcast_to(inner_part, (8, 128))
+    for k in far_z:
+        go(i_tile(k))
+
     for k in range(1, N):
         z_tile(k).wait_recv()
-    sums = zt[0]
-    for i in range(1, N):
-        sums = sums + zt[i]
-    weight = jnp.exp(sums[0:1])
-    inner = sums[1:2]
+    score = zt[0, 0:1]
+    for i in range(1, N):
+        score = score + zt[i, 0:1]
+    weight = jnp.exp(score)
     risk = jnp.full((1, 128), cost_ref[0, 0], jnp.int32).astype(F32) / 100.0
     ct[c] = jnp.where(line == 0, weight, jnp.where(line == 1, risk, 0.0))
-    for k in range(1, N):
+    for k in far_c:
         go(c_tile(k))
+    drain(4 * N)
 
     rs_round(3)
 
@@ -384,9 +410,6 @@
         total_w = total_w + ct[i, 0:1]
         total_wr = total_wr + ct[i, 0:1] * ct[i, 1:2]
     expected = total_wr / total_w
-    lt[s] = jnp.broadcast_to(expected, (8, 128))
-    for k in range(1, N):
-        go(l_tile(k))
     dkr[c] = dks[c]
     for k in range(1, N):
         dk1(k).wait_recv()
@@ -395,9 +418,13 @@
         share = ct[i, 0:1] / total_w * (ct[i, 1:2] - expected) / N
         total = total + share * dkr[i].astype(F32)
     dko[c] = total.astype(BF)
-    for k in range(1, N):
+    for k in far_c:
         go(dk2(k))
-
+    lt[s] = jnp.broadcast_to(expected, (8, 128))
+    for k in range(1, N):
+        go(l_tile(k))
+
+    drain(2 * N)
     rs_round(2)
 
     for k in range(1, N):
@@ -409,26 +436,18 @@
     enc_term = enc_term + dot_tt(jnp.concatenate(sides[2:], axis=1), wv_ref[...])
     for i in range(N):
         ens[i] = enc_term[i * gpad : (i + 1) * gpad].astype(BF)
-    for k in range(1, N):
+    for k in far_z:
         go(en(k))
+    enr[z] = ens[z]
+    drain(2 * N)
 
     rs_round(1)
 
-    enr[z] = ens[z]
-    for k in range(1, N):
-        en(k).wait_recv()
-    total = enr[0].astype(F32)
-    for i in range(1, N):
-        total = total + enr[i].astype(F32)
-    genc_ref[...] = total[:group]
-
-    for k in range(1, N):
-        l_tile(k).wait_recv()
-    loss = lt[0, 0:1]
-    for i in range(1, N):
-        loss = loss + lt[i, 0:1]
-    loss_ref[...] = loss / N
-
+    for k in range(1, N):
+        i_tile(k).wait_recv()
+    inner = it[0, 0:1]
+    for i in range(1, N):
+        inner = inner + it[i, 0:1]
     share = weight / total_w * (risk - expected) / N
     rad_ref[...] = share * inner / jnp.sqrt(jnp.full((1, 128), width, F32))
     share_col = share[:, 0:1]
@@ -444,8 +463,19 @@
         + inv_rms * gain_part * normed_grad
         - x_part * (inv_rms * inv_rms * inv_rms * inner_col / width)
     )
-    for copy in started:
-        copy.wait_send()
+    for k in range(1, N):
+        l_tile(k).wait_recv()
+    loss = lt[0, 0:1]
+    for i in range(1, N):
+        loss = loss + lt[i, 0:1]
+    loss_ref[...] = loss / N
+    for k in range(1, N):
+        en(k).wait_recv()
+    total = enr[0].astype(F32)
+    for i in range(1, N):
+        total = total + enr[i].astype(F32)
+    genc_ref[...] = total[:group]
+    drain()
 
 
 def local(
@@ -494,15 +524,17 @@
             pltpu.VMEM((N, 8, 128), F32),
             pltpu.VMEM((N, 8, 128), F32),
             pltpu.VMEM((N, 8, 128), F32),
+            pltpu.VMEM((N, 8, 128), F32),
             pltpu.VMEM((N, gpad, depth), BF),
             pltpu.VMEM((N, gpad, depth), BF),
             pltpu.VMEM((2, 4, tgt, wide), BF),
             pltpu.VMEM((2, 4, tgt, wide), BF),
             pltpu.VMEM((2, tgt, wide), F32),
+            dma((N,)), dma((N,)),
             dma((2, 4, CH)), dma((2, 4, CH)),
-            dma((2, 3)), dma((2, 3)),
-            dma((2, 4)), dma((2, 4)),
-            dma((2, 7)), dma((2, 7)),
+            dma((2 * WCH, 4)), dma((2 * WCH, 4)),
+            dma((2 * WCH, 4)), dma((2 * WCH, 4)),
+            dma((2 * WCH, 7)), dma((2 * WCH, 7)),
         ]
         + [dma((N,))] * 16
         + [dma((2, 4, CH)), dma((2, 4, CH))],

time: 64.9 us -> 62.3 us (0.960)
  Pallas kernels: 59.1 us -> 56.6 us
    pallas_call x1, Pallas kernels: 59.1 us -> 56.6 us  [local(): pl.pallas_call(kernel, out_shape=(jax.ShapeDtypeStruct((1, 128), F32), ja...]
where the time goes in v3:
time: 62.3 us; the launch traced here: 62.2 us
  Pallas kernels  56.6 us (91%)
  between operations  3.75 us (6%)
  local copies, waits for them, and re-layouts  1.85 us (3%)
    pallas_call x1, Pallas kernels, local(): pl.pallas_call(kernel, out_shape=(jax.ShapeDtypeStruct((1, 128), F32), ja...  56.6 us
    unnamed x3, local copies, waits for them, and re-layouts  1.85 us

profile of v3, /device:TPU:8, one launch (start us, length us, event | category | flops | bytes accessed | tf_op | source)
XLA Modules:
  0.0 62.2 jit_solution(15602562784410981119)
XLA Ops:
  2.6 56.6 %shard_map.138 = (f32[1,128]{1,0:T(1,128)S(1)}, f32[128,512]{1,0:T(8,128)S(1)}, f32[12,512]{1,0:T(8,128)S(1)}, f32[1,128]{1,0:T(1,128)S(1)}) custom-call(bf16[128,512]{1,0:T(8,128)(2,1)} %bitcast.14, bf16[96,512]{1,0:T(8,128)(2,1)} %bitcast.15, f32[1,4096]{1,0:T(1,128)} %bitcast.16, bf16[512,256]{1,0:T(8,128)(2,1)} %wq_in.1, bf16[512,256]{1,0:T(8,128)(2,1)} %wk_in.1, ...), custom_call_target="tpu_custom_call" | custom-call | tf_op jit(solution)/shard_map/pallas_call | solution.py:496
  59.2 0.6 %copy.15 = f32[1,12,512]{2,0,1:T(1,128)} copy(f32[1,12,512]{2,1,0:T(8,128)S(1)} %bitcast.10) | data formatting | bytes 49152
  59.8 0.7 %copy.23 = f32[1,1,128,512]{3,2,1,0:T(8,128)} copy(f32[1,1,128,512]{3,2,1,0:T(8,128)S(1)} %bitcast.9) | data formatting | bytes 524288
  60.5 0.5 copy.24

commit v4 on v3

--- a/solution.py
+++ b/solution.py
@@ -60,6 +60,12 @@
     y_to = {"source": up(s, 2 * yl * (1 - core) - 2 * (1 - yl) * core), "cand": c + 1 - 2 * yl}
     y_from = {"source": up(s, 2 * yl * core - 2 * (1 - yl) * (1 - core)), "cand": c + 1 - 2 * yl}
 
+    barrier = pltpu.get_barrier_semaphore()
+    for k in range(1, N):
+        pl.semaphore_signal(barrier, inc=1, device_id={"tensor": up(z, k)}, device_id_type=MESH)
+        pl.semaphore_signal(barrier, inc=1, device_id={"cand": up(c, k)}, device_id_type=MESH)
+        pl.semaphore_signal(barrier, inc=1, device_id={"source": up(s, k)}, device_id_type=MESH)
+    pl.semaphore_signal(barrier, inc=1, device_id=y_from, device_id_type=MESH)
     x_own, wq_own, wo_own = xg.at[z], wqf.at[c], wof.at[c]
     into = (x_own, wq_own, enc_ref, wk_ref, wv_ref, wo_own, rows_ref, gain_ref)
     local_copies = [
@@ -69,13 +75,6 @@
     for copy in local_copies:
         copy.start()
     x_load, wq_load, enc_load, wk_load, wv_load, wo_load, rows_load, gain_load = local_copies
-
-    barrier = pltpu.get_barrier_semaphore()
-    for k in range(1, N):
-        pl.semaphore_signal(barrier, inc=1, device_id={"tensor": up(z, k)}, device_id_type=MESH)
-        pl.semaphore_signal(barrier, inc=1, device_id={"cand": up(c, k)}, device_id_type=MESH)
-        pl.semaphore_signal(barrier, inc=1, device_id={"source": up(s, k)}, device_id_type=MESH)
-    pl.semaphore_signal(barrier, inc=1, device_id=y_from, device_id_type=MESH)
     pl.semaphore_wait(barrier, 3 * (N - 1) + 1)
 
     started = []
@@ -230,6 +229,9 @@
 
     def r_term(b):
         return dot_tt(rows_ref[:, pl.ds(pl.multiple_of(b * wide, wide), wide)], wof[b])
+
+    def q_term(b):
+        return dot(xn[:, pl.ds(pl.multiple_of(b * wide, wide), wide)], wqf[b])
 
     wq_load.wait()
     wo_load.wait()
@@ -261,25 +263,27 @@
         w_got(1, i)
     back = back + r_term(piece(0, 1)) + r_term(piece(1, 0)) + r_term(piece(-1, 0))
     x_round(4)
-    squares = squares + gained(up(z, 3)) + gained(up(z, -3))
+    squares = squares + gained(up(z, 3)) + gained(up(z, -3)) + gained(up(z, 4))
+    for i in (1, 2, 4):
+        w_got(0, i)
+    q_raw = q_term(c) + q_term(piece(0, 1)) + q_term(piece(1, 0)) + q_term(piece(-1, 0))
     w_end(0)
+    w_end(1)
     w_got(1, 3)
-    back = back + r_term(piece(2, 0))
     w_got(1, 5)
     w_got(1, 6)
-    back = back + r_term(piece(1, 1)) + r_term(piece(-1, 1))
-    w_end(1)
-    squares = squares + gained(up(z, 4))
+    back = back + r_term(piece(2, 0)) + r_term(piece(1, 1)) + r_term(piece(-1, 1))
+    w_got(0, 3)
+    w_got(0, 5)
+    w_got(0, 6)
+    q_raw = q_raw + q_term(piece(2, 0)) + q_term(piece(1, 1)) + q_term(piece(-1, 1))
     for k in range(1, N):
         kv2(k).wait_recv()
     for g in range(4):
         for r in range(2):
             kvf[r * (pad // 2) : (r + 1) * (pad // 2), g * 128 : (g + 1) * 128] = kvo[g * 2 + r]
-    for i in range(1, N):
-        w_got(0, i)
-    q_raw = jnp.zeros((tgt, cols), F32)
-    for b in range(N):
-        q_raw = q_raw + dot(xn[:, b * wide : (b + 1) * wide], wqf[b])
+    w_got(0, 7)
+    q_raw = q_raw + q_term(piece(2, 1))
     inv_rms = lax.rsqrt(squares / width + 1e-06)
     query = (q_raw * inv_rms).astype(BF)
     w_got(1, 7)
@@ -440,7 +444,6 @@
         go(en(k))
     enr[z] = ens[z]
     drain(2 * N)
-
     rs_round(1)
 
     for k in range(1, N):
@@ -452,17 +455,15 @@
     rad_ref[...] = share * inner / jnp.sqrt(jnp.full((1, 128), width, F32))
     share_col = share[:, 0:1]
     inner_col = jnp.sum(jnp.where(eye, inner, 0.0), axis=1, keepdims=True)
+    gain_part = gain_ref[:, pl.ds(pl.multiple_of(z * wide, wide), wide)]
+    gdec_ref[...] = share_col * (factor * rows_part - x_part * (inv_rms * inv_rms * inv_rms * inner_col / width))
     own[0] = term(z)
+    own[1] = (share_col * inv_rms) * gain_part
     for chunk in range(CH):
         for way in range(2):
             rs_copy(way, 1, chunk).wait_recv()
     normed_grad = own[0] + rsr[0, 0].astype(F32) + rsr[1, 0].astype(F32)
-    gain_part = gain_ref[:, pl.ds(pl.multiple_of(z * wide, wide), wide)]
-    gdec_ref[...] = share_col * (
-        factor * rows_part
-        + inv_rms * gain_part * normed_grad
-        - x_part * (inv_rms * inv_rms * inv_rms * inner_col / width)
-    )
+    gdec_ref[...] = gdec_ref[...] + own[1] * normed_grad
     for k in range(1, N):
         l_tile(k).wait_recv()
     loss = lt[0, 0:1]

time: 62.3 us -> 61.9 us (level)
  no operation moved by 1% of the time
where the time goes in v4:
time: 61.9 us; the launch traced here: 61.8 us
  Pallas kernels  56.2 us (91%)
  between operations  3.75 us (6%)
  local copies, waits for them, and re-layouts  1.85 us (3%)
    pallas_call x1, Pallas kernels, local(): pl.pallas_call(kernel, out_shape=(jax.ShapeDtypeStruct((1, 128), F32), ja...  56.2 us
    unnamed x3, local copies, waits for them, and re-layouts  1.85 us

profile of v4, /device:TPU:8, one launch (start us, length us, event | category | flops | bytes accessed | tf_op | source)
XLA Modules:
  0.0 61.8 jit_solution(6052721603307933935)
XLA Ops:
  2.6 56.2 %shard_map.138 = (f32[1,128]{1,0:T(1,128)S(1)}, f32[128,512]{1,0:T(8,128)S(1)}, f32[12,512]{1,0:T(8,128)S(1)}, f32[1,128]{1,0:T(1,128)S(1)}) custom-call(bf16[128,512]{1,0:T(8,128)(2,1)} %bitcast.14, bf16[96,512]{1,0:T(8,128)(2,1)} %bitcast.15, f32[1,4096]{1,0:T(1,128)} %bitcast.16, bf16[512,256]{1,0:T(8,128)(2,1)} %wq_in.1, bf16[512,256]{1,0:T(8,128)(2,1)} %wk_in.1, ...), custom_call_target="tpu_custom_call" | custom-call | tf_op jit(solution)/shard_map/pallas_call | solution.py:497
  58.8 0.6 %copy.15 = f32[1,12,512]{2,0,1:T(1,128)} copy(f32[1,12,512]{2,1,0:T(8,128)S(1)} %bitcast.10) | data formatting | bytes 49152
  59.4 0.7 %copy.23 = f32[1,1,128,512]{3,2,1,0:T(8,128)} copy(f32[1,1,128,512]{3,2,1,0:T(8,128)S(1)} %bitcast.9) | data formatting | bytes 524288
  60.1 0.5 copy.24

commit v5 on v4

--- a/solution.py
+++ b/solution.py
@@ -181,11 +181,11 @@
             go(w_own(m, i))
         go(w_y(m, 0))
 
+    for m in range(2 * WCH):
+        w_start(m)
     for chunk in range(CH):
         for way in range(2):
             go(x_copy(way, 1, chunk))
-    for m in range(2 * WCH):
-        w_start(m)
 
     row = lax.broadcasted_iota(jnp.int32, (pad, srcs), 0)
     col = lax.broadcasted_iota(jnp.int32, (pad, srcs), 1)
@@ -323,8 +323,12 @@
     def c_tile(k):
         return remote(ct.at[c], ct.at[c], css.at[k], csr.at[k], {"cand": up(c, k)})
 
+    def l_pair():
+        return remote(lt.at[core], lt.at[core], lss.at[0], lsr.at[0], {"source": s + sgn})
+
     def l_tile(k):
-        return remote(lt.at[s], lt.at[s], lss.at[k], lsr.at[k], {"source": up(s, k)})
+        there = lt.at[2 + s // 2]
+        return remote(there, there, lss.at[k], lsr.at[k], {"source": up(s, 2 * k)})
 
     def dk1(k):
         return cand_all(lambda i: dks.at[i], dkr, d1s, d1r, k)
@@ -424,9 +428,8 @@
     dko[c] = total.astype(BF)
     for k in far_c:
         go(dk2(k))
-    lt[s] = jnp.broadcast_to(expected, (8, 128))
-    for k in range(1, N):
-        go(l_tile(k))
+    lt[core] = jnp.broadcast_to(expected, (8, 128))
+    go(l_pair())
 
     drain(2 * N)
     rs_round(2)
@@ -443,6 +446,10 @@
     for k in far_z:
         go(en(k))
     enr[z] = ens[z]
+    l_pair().wait_recv()
+    lt[2 + s // 2] = lt[0] + lt[1]
+    for k in range(1, N // 2):
+        go(l_tile(k))
     drain(2 * N)
     rs_round(1)
 
@@ -464,10 +471,10 @@
             rs_copy(way, 1, chunk).wait_recv()
     normed_grad = own[0] + rsr[0, 0].astype(F32) + rsr[1, 0].astype(F32)
     gdec_ref[...] = gdec_ref[...] + own[1] * normed_grad
-    for k in range(1, N):
+    for k in range(1, N // 2):
         l_tile(k).wait_recv()
-    loss = lt[0, 0:1]
-    for i in range(1, N):
+    loss = lt[2, 0:1]
+    for i in range(3, 2 + N // 2):
         loss = loss + lt[i, 0:1]
     loss_ref[...] = loss / N
     for k in range(1, N):

time: 61.9 us -> 61.9 us (level)
  no operation moved by 1% of the time
where the time goes in v5:
time: 61.9 us; the launch traced here: 61.7 us
  Pallas kernels  56.1 us (91%)
  between operations  3.75 us (6%)
  local copies, waits for them, and re-layouts  1.85 us (3%)
    pallas_call x1, Pallas kernels, local(): pl.pallas_call(kernel, out_shape=(jax.ShapeDtypeStruct((1, 128), F32), ja...  56.1 us
    unnamed x3, local copies, waits for them, and re-layouts  1.85 us

profile of v5, /device:TPU:8, one launch (start us, length us, event | category | flops | bytes accessed | tf_op | source)
XLA Modules:
  0.0 61.7 jit_solution(13075039649098653504)
XLA Ops:
  2.6 56.1 %shard_map.138 = (f32[1,128]{1,0:T(1,128)S(1)}, f32[128,512]{1,0:T(8,128)S(1)}, f32[12,512]{1,0:T(8,128)S(1)}, f32[1,128]{1,0:T(1,128)S(1)}) custom-call(bf16[128,512]{1,0:T(8,128)(2,1)} %bitcast.14, bf16[96,512]{1,0:T(8,128)(2,1)} %bitcast.15, f32[1,4096]{1,0:T(1,128)} %bitcast.16, bf16[512,256]{1,0:T(8,128)(2,1)} %wq_in.1, bf16[512,256]{1,0:T(8,128)(2,1)} %wk_in.1, ...), custom_call_target="tpu_custom_call" | custom-call | tf_op jit(solution)/shard_map/pallas_call | solution.py:504
  58.7 0.6 %copy.15 = f32[1,12,512]{2,0,1:T(1,128)} copy(f32[1,12,512]{2,1,0:T(8,128)S(1)} %bitcast.10) | data formatting | bytes 49152
  59.4 0.7 %copy.23 = f32[1,1,128,512]{3,2,1,0:T(8,128)} copy(f32[1,1,128,512]{3,2,1,0:T(8,128)S(1)} %bitcast.9) | data formatting | bytes 524288
  60.1 0.5 copy.24
